TPU v7x, 32 devices: a whole 2x2x4 slice. The times are simulated.
32 devices in a mesh: dp: 4 (over y, x), expert: 4 (over z), tensor: 2 (over core).
Axes of the slice: x: 2, y: 2, z: 4, core: 2. Of those that a mesh axis runs over, the one named last changes fastest.
Arguments:
- tokens: bfloat16 [2048, 4096], P('expert', 'dp'), may hold values from -6 to 6
- labels: int32 [2048, 1], P('expert'), may hold values from 0 to 7; in each aligned block of 512 rows (0 to 511, 512 to 1023, ...) at most 96 rows name the same one
- grad_out: bfloat16 [2048, 4096], P('expert', 'dp'), may hold values from -1.5 to 1.5
- w_gate: bfloat16 [8, 4096, 7168], P('expert', 'dp', 'tensor'), may hold values from -0.09375 to 0.09375
- w_up: bfloat16 [8, 4096, 7168], P('expert', 'dp', 'tensor'), may hold values from -0.09375 to 0.09375
- w_down: bfloat16 [8, 7168, 4096], P('expert', 'tensor', 'dp'), may hold values from -0.0625 to 0.0625
Outputs:
- mixed: bfloat16 [2048, 4096], P('expert', 'dp')
- grad_tokens: bfloat16 [2048, 4096], P('expert', 'dp')
- grad_gate: bfloat16 [8, 4096, 7168], P('expert', 'dp', 'tensor')
- grad_up: bfloat16 [8, 4096, 7168], P('expert', 'dp', 'tensor')
- grad_down: bfloat16 [8, 7168, 4096], P('expert', 'tensor', 'dp')
Inputs may be any that keep to these rules, and one draw needn't show every extreme that they name: `labels`: in each aligned block of 512 rows (the rows of one index of expert) no domain appears more than 96 times; some domain appears exactly 96 times in some block. Every domain appears somewhere.
All inputs are finite; a program needn't handle non-finite values.
Results may differ from a plain program's by a relative error of at most 0.005.
Values may be sent and summed in bfloat16 or wider, within the bound.
No kernel may reach another device: no remote copies, remote signals or barrier semaphores. Data moves between devices by JAX's collectives and lax.ppermute only.
A program may use at most 192 MiB of HBM per device.

v0:
```python
import jax
import jax.numpy as jnp
from jax import lax
from jax.sharding import PartitionSpec as P

MOST = 96


def body(tokens, labels, grad_out, w_gate, w_up, w_down):
    local_experts = w_gate.shape[0]
    groups = lax.axis_size("expert")
    experts = local_experts * groups
    feat_width = tokens.shape[1]
    hidden_width = w_gate.shape[2]
    domain = labels[:, 0]
    onehot = (domain[:, None] == jnp.arange(experts, dtype=jnp.int32)[None, :]).astype(jnp.int32)
    before = jnp.cumsum(onehot, axis=0) - onehot
    rank_in = jnp.sum(before * onehot, axis=1)
    slot_of = rank_in * experts + domain
    positions = jnp.arange(experts * MOST, dtype=jnp.int32)
    to_slots = (positions[:, None] == slot_of[None, :]).astype(jnp.bfloat16)
    from_slots = (slot_of[:, None] == positions[None, :]).astype(jnp.bfloat16)
    payload = jnp.concatenate([tokens, grad_out], axis=1)
    packed = jnp.dot(to_slots, payload, preferred_element_type=jnp.float32).astype(jnp.bfloat16)
    packed = packed.reshape(MOST, groups, local_experts, 2 * feat_width)
    arrived = lax.all_to_all(packed, "expert", split_axis=1, concat_axis=1, tiled=True)
    inputs = arrived[..., :feat_width]
    grad_rows = arrived[..., feat_width:]
    gate_part = jnp.einsum("msjd,jdf->msjf", inputs, w_gate, preferred_element_type=jnp.float32)
    up_part = jnp.einsum("msjd,jdf->msjf", inputs, w_up, preferred_element_type=jnp.float32)
    back_part = jnp.einsum("msjd,jfd->msjf", grad_rows, w_down, preferred_element_type=jnp.float32)
    scattered = lax.psum_scatter(
        jnp.concatenate([gate_part, up_part, back_part], axis=-1),
        "dp",
        scatter_dimension=0,
        tiled=True,
    )
    gate_sum = scattered[..., :hidden_width]
    up_sum = scattered[..., hidden_width : 2 * hidden_width]
    back_sum = scattered[..., 2 * hidden_width :]
    sigmoid_gate = jax.nn.sigmoid(gate_sum)
    active = gate_sum * sigmoid_gate
    hidden_act = (active * up_sum).astype(jnp.bfloat16)
    d_gate = (back_sum * up_sum * (sigmoid_gate * (1.0 + gate_sum * (1.0 - sigmoid_gate)))).astype(
        jnp.bfloat16
    )
    d_up = (back_sum * active).astype(jnp.bfloat16)
    local_acts = jnp.concatenate([hidden_act, d_gate, d_up], axis=-1)
    act_rows = lax.all_gather(local_acts, "dp", axis=0, tiled=True)
    inputs = arrived[..., :feat_width]
    grad_rows = arrived[..., feat_width:]
    act_piece = act_rows[..., :hidden_width]
    gate_piece = act_rows[..., hidden_width : 2 * hidden_width]
    up_piece = act_rows[..., 2 * hidden_width :]
    forward = jnp.einsum("msjf,jfd->msjd", act_piece, w_down, preferred_element_type=jnp.float32)
    backward = jnp.einsum("msjf,jdf->msjd", gate_piece, w_gate, preferred_element_type=jnp.float32)
    backward = backward + jnp.einsum(
        "msjf,jdf->msjd", up_piece, w_up, preferred_element_type=jnp.float32
    )
    rows_out = jnp.concatenate([forward, backward], axis=-1)
    down_acc = jnp.einsum(
        "msjf,msjd->jfd", act_piece, grad_rows, preferred_element_type=jnp.float32
    )
    gate_acc = jnp.einsum("msjd,msjf->jdf", inputs, gate_piece, preferred_element_type=jnp.float32)
    up_acc = jnp.einsum("msjd,msjf->jdf", inputs, up_piece, preferred_element_type=jnp.float32)
    rows_out, down_acc, gate_acc, up_acc = (rows_out, down_acc, gate_acc, up_acc)
    shares_part = lax.psum_scatter(rows_out, "tensor", scatter_dimension=3, tiled=True).astype(
        jnp.bfloat16
    )
    returned = lax.all_to_all(shares_part, "expert", split_axis=1, concat_axis=1, tiled=True)
    home_rows = lax.all_gather(returned, "tensor", axis=3, tiled=True)
    home_flat = home_rows.reshape(experts * MOST, 2 * feat_width)
    result = jnp.dot(from_slots, home_flat, preferred_element_type=jnp.float32).astype(jnp.bfloat16)
    mixed_rows = result[:, :feat_width]
    grad_rows_home = result[:, feat_width:]
    return (
        mixed_rows,
        grad_rows_home,
        gate_acc.astype(jnp.bfloat16),
        up_acc.astype(jnp.bfloat16),
        down_acc.astype(jnp.bfloat16),
    )


def solution(mesh):
    in_specs = (
        P("expert", "dp"),
        P("expert", None),
        P("expert", "dp"),
        P("expert", "dp", "tensor"),
        P("expert", "dp", "tensor"),
        P("expert", "tensor", "dp"),
    )
    out_specs = (
        P("expert", "dp"),
        P("expert", "dp"),
        P("expert", "dp", "tensor"),
        P("expert", "dp", "tensor"),
        P("expert", "tensor", "dp"),
    )
    return jax.shard_map(body, mesh=mesh, in_specs=in_specs, out_specs=out_specs, check_vma=False)
```

profile of v0, /device:TPU:11, one launch (start us, length us, event | category | flops | bytes accessed | tf_op | source)
XLA Modules:
  0.0 780.9 jit_solution(9501737769938717962)
XLA Ops:
  10.7 5.0 convolution_convert_fusion
  15.7 6.0 reshape.50
  21.7 3.8 copy.14
  25.5 73.3 %all_to_all.10 = bf16[96,4,2,2048]{3,0,2,1:T(8,128)(2,1)S(1)} all-to-all(bf16[96,4,2,2048]{3,0,2,1:T(8,128)(2,1)S(1)} %copy.14), channel_id=1, replica_groups=mesh['dp'=4,'expert'=4,'tensor'=2] {'expert'}, dimensions={1} | all-to-all | bytes 6291456 | tf_op jit(solution)/shard_map/all_to_all | solution.py:26
  99.1 8.6 %fusion.15 = f32[96,4,2,3584]{3,0,1,2:T(8,128)} fusion(bf16[2,1024,3584]{2,1,0:T(8,128)(2,1)S(1)} %copy-done, bf16[96,4,2,1024]{3,0,2,1:T(8,128)(2,1)S(1)} %get-tuple-element.8), kind=kOutput, calls=%fused_computation.17 | convolution fusion | flops 5637144576 | bytes 27262976 | tf_op jit(solution)/shard_map/msjd,jdf->msjf/dot_general | solution.py:30
  107.7 13.7 %fusion.12 = f32[96,4,2,3584]{3,0,1,2:T(8,128)} fusion(bf16[2,1024,3584]{2,1,0:T(8,128)(2,1)} %param.9, bf16[96,4,2,1024]{3,0,2,1:T(8,128)(2,1)S(1)} %get-tuple-element.8), kind=kOutput, calls=%fused_computation.16 | convolution fusion | flops 5637144576 | bytes 27262976 | tf_op jit(solution)/shard_map/msjd,jdf->msjf/dot_general | solution.py:29
  121.4 21.7 %fusion.18 = f32[96,4,2,3584]{3,0,1,2:T(8,128)} fusion(bf16[2,3584,1024]{2,1,0:T(8,128)(2,1)} %param.11, bf16[96,4,2,1024]{3,0,2,1:T(8,128)(2,1)S(1)} %get-tuple-element.9), kind=kOutput, calls=%fused_computation.18 | convolution fusion | flops 5637144576 | bytes 27262976 | tf_op jit(solution)/shard_map/msjd,jfd->msjf/dot_general | solution.py:31
  143.1 22.6 %pad_maximum_fusion = f32[96,4,2,10752]{3,0,1,2:T(8,128)} fusion(f32[96,4,2,3584]{3,0,1,2:T(8,128)} %fusion.18, f32[96,4,2,3584]{3,0,1,2:T(8,128)} %fusion.15, f32[96,4,2,3584]{3,0,1,2:T(8,128)} %fusion.12), kind=kLoop, calls=%fused_computation | loop fusion | flops 16515072 | bytes 66060288 | tf_op jit(solution)/shard_map/concatenate | solution.py:33
  165.7 286.4 %reduce-scatter.3.cloned.1.call-done = f32[24,4,2,10752]{3,0,1,2:T(8,128)} async-done(((f32[96,4,2,10752]{3,0,1,2:T(8,128)}), f32[24,4,2,10752]{3,0,1,2:T(8,128)}) %reduce-scatter.3.cloned.1.call-update) | async-done | bytes 8257552 | tf_op jit(solution)/shard_map/reduce_scatter | solution.py:32
  452.2 4.1 multiply_convert_fusion.2
  458.7 155.3 %all-gather.3.cloned.1.call-done = bf16[96,4,2,10752]{3,0,1,2:T(8,128)(2,1)} async-done(((bf16[24,4,2,10752]{3,0,1,2:T(8,128)(2,1)}), bf16[96,4,2,10752]{3,0,1,2:T(8,128)(2,1)}) %all-gather.3.cloned.1.call-update) | async-done | bytes 16515088 | tf_op jit(solution)/shard_map/all_gather | solution.py:49
  614.0 11.9 %fusion.4 = f32[2,96,4,1024]{3,1,2,0:T(8,128)} fusion(bf16[2,1024,3584]{2,1,0:T(8,128)(2,1)} %param.10, bf16[96,4,2,10752]{3,0,1,2:T(8,128)(2,1)} %all-gather.3.cloned.1.call-done), kind=kOutput, calls=%fused_computation.8 | convolution fusion | flops 5637144576 | bytes 23330816 | tf_op jit(solution)/shard_map/msjf,jdf->msjd/dot_general | solution.py:57
  625.9 13.2 %fusion.31 = f32[96,4,2,1024]{3,0,1,2:T(8,128)} fusion(bf16[2,3584,1024]{2,1,0:T(8,128)(2,1)} %param.11, bf16[96,4,2,10752]{3,0,1,2:T(8,128)(2,1)} %all-gather.3.cloned.1.call-done), kind=kOutput, calls=%fused_computation.38 | convolution fusion | flops 5637144576 | bytes 23330816 | tf_op jit(solution)/shard_map/msjf,jfd->msjd/dot_general | solution.py:55
  639.1 12.3 %add_bitcast_fusion = f32[96,4,2,1024]{3,0,1,2:T(8,128)} fusion(f32[2,96,4,1024]{3,1,2,0:T(8,128)} %fusion.4, bf16[2,1024,3584]{2,1,0:T(8,128)(2,1)} %param.9, bf16[96,4,2,10752]{3,0,1,2:T(8,128)(2,1)} %all-gather.3.cloned.1.call-done), kind=kOutput, calls=%fused_computation.28 | convolution fusion | flops 5637931008 | bytes 26476544 | tf_op jit(solution)/shard_map/msjf,jdf->msjd/dot_general | solution.py:56
  651.5 6.3 pad_maximum_fusion.1
  657.9 15.4 %reduce-scatter.5.cloned.1.call-done = f32[96,4,2,1024]{3,0,1,2:T(8,128)} async-done(((f32[96,4,2,2048]{3,0,1,2:T(8,128)}), f32[96,4,2,1024]{3,0,1,2:T(8,128)}) %reduce-scatter.5.cloned.1.call-update) | async-done | bytes 3145744 | tf_op jit(solution)/shard_map/reduce_scatter | solution.py:67
  676.7 4.6 all-to-all-start.1
  681.5 33.4 %all-to-all-done.1 = bf16[96,4,2,1024]{3,0,2,1:T(8,128)(2,1)} async-done(((bf16[96,4,2,1024]{3,0,2,1:T(8,128)(2,1)}), bf16[96,4,2,1024]{3,0,2,1:T(8,128)(2,1)}, u32[]{:S(2)}, u32[]{:S(2)}) %all-to-all-start.1) | async-done | bytes 1572896 | tf_op jit(solution)/shard_map/all_to_all | solution.py:70
  714.9 14.0 %bitcast_convert_fusion = bf16[2,3584,1024]{2,1,0:T(8,128)(2,1)} fusion(bf16[96,4,2,10752]{3,0,1,2:T(8,128)(2,1)} %all-gather.3.cloned.1.call-done, bf16[96,4,2,1024]{3,0,2,1:T(8,128)(2,1)S(1)} %get-tuple-element.9), kind=kOutput, calls=%fused_computation.1 | convolution fusion | flops 5644484608 | bytes 21757952 | tf_op jit(solution)/shard_map/msjf,msjd->jfd/dot_general | solution.py:61
  728.8 13.7 %bitcast_convert_fusion.2 = bf16[2,1024,3584]{2,1,0:T(8,128)(2,1)} fusion(bf16[96,4,2,10752]{3,0,1,2:T(8,128)(2,1)} %all-gather.3.cloned.1.call-done, bf16[96,4,2,1024]{3,0,2,1:T(8,128)(2,1)S(1)} %get-tuple-element.8), kind=kOutput, calls=%fused_computation.3 | convolution fusion | flops 5644484608 | bytes 21757952 | tf_op jit(solution)/shard_map/msjd,msjf->jdf/dot_general | solution.py:64
  742.5 13.9 %bitcast_convert_fusion.1 = bf16[2,1024,3584]{2,1,0:T(8,128)(2,1)} fusion(bf16[96,4,2,10752]{3,0,1,2:T(8,128)(2,1)} %all-gather.3.cloned.1.call-done, bf16[96,4,2,1024]{3,0,2,1:T(8,128)(2,1)S(1)} %get-tuple-element.8), kind=kOutput, calls=%fused_computation.2 | convolution fusion | flops 5644484608 | bytes 21757952 | tf_op jit(solution)/shard_map/msjd,msjf->jdf/dot_general | solution.py:65
  756.4 6.8 copy.18
  763.2 5.7 reshape.51
  768.9 3.7 convolution_convert_fusion.1
  (26 shorter events, 11.5 us)
Async XLA Ops:
  7.2 445.0 %reduce-scatter.3.cloned.1.call-start = ((), (), s32[]{:S(2)}) async-start(), calls=%async_computation.4 | async-start | bytes 41287680 | tf_op jit(solution)/shard_map/reduce_scatter | solution.py:32
  21.7 77.4 %copy-start = (bf16[2,1024,3584]{2,1,0:T(8,128)(2,1)S(1)}, bf16[2,1024,3584]{2,1,0:T(8,128)(2,1)}, u32[]{:S(2)}) copy-start(bf16[2,1024,3584]{2,1,0:T(8,128)(2,1)} %param.10) | copy-start | bytes 44040196
  165.7 448.3 %all-gather.3.cloned.1.call-start = ((), (), s32[]{:S(2)}) async-start(), calls=%async_computation.5 | async-start | bytes 20643840 | tf_op jit(solution)/shard_map/all_gather | solution.py:49
  458.5 214.8 %reduce-scatter.5.cloned.1.call-start = ((), (), s32[]{:S(2)}) async-start(), calls=%async_computation.6 | async-start | bytes 9437184 | tf_op jit(solution)/shard_map/reduce_scatter | solution.py:67
  675.4 6.1 copy-start.1
  676.7 38.2 %all-to-all-start.1 = ((bf16[96,4,2,1024]{3,0,2,1:T(8,128)(2,1)}), bf16[96,4,2,1024]{3,0,2,1:T(8,128)(2,1)}, u32[]{:S(2)}, u32[]{:S(2)}) async-start(bf16[96,4,2,1024]{3,0,2,1:T(8,128)(2,1)} %copy.17), calls=%async_computation.3 | async-start | bytes 3145728 | tf_op jit(solution)/shard_map/all_to_all | solution.py:70
  681.2 75.1 %all-gather.5.cloned.1.call-start = ((), (), s32[]{:S(2)}) async-start(), calls=%async_computation.7 | async-start | bytes 4718592 | tf_op jit(solution)/shard_map/all_gather | solution.py:71
Sparse Core Ops, SparseCore 0:
  165.8 286.3 reduce-scatter.2
  458.6 155.3 all-gather.2
  658.0 15.2 reduce-scatter.4
  715.0 15.3 all-gather.4
where the time goes:
time: 790 us; the launch traced here: 781 us
  waiting for transfers between devices  491 us (62%)
  matrix products  132 us (17%)
  blocking collectives  73.3 us (9%)
  other arithmetic  40.6 us (5%)
  local copies, waits for them, and re-layouts  25.6 us (3%)
  between operations  14.1 us (2%)
    reduce_scatter x1, waiting for transfers between devices, body(): lax.psum_scatter(jnp.concatenate([gate_part, up_part, back_part], axis=-1...  286 us
    all_gather x1, waiting for transfers between devices, body(): act_rows = lax.all_gather(local_acts, 'dp', axis=0, tiled=True)  155 us
    all_to_all x1, blocking collectives, body(): lax.all_to_all(packed, 'expert', split_axis=1, concat_axis=1, tiled=True)  73.3 us
    all_to_all x1, waiting for transfers between devices, body(): lax.all_to_all(shares_part, 'expert', split_axis=1, concat_axis=1, tiled=...  33.4 us
    concatenate x1, other arithmetic, body(): jnp.concatenate([gate_part, up_part, back_part], axis=-1)  22.6 us
    dot_general x1, matrix products, body(): jnp.einsum('msjd,jfd->msjf', grad_rows, w_down, preferred_element_type=jn...  21.7 us
  transfers between devices with their start and end apart: 5, of which 4 were waited for; matrix products, arithmetic and copies ran while one was open for 5% of the time, Pallas kernels for 0%

commit v1 on v0

v1 whole, which is shorter than its diff:
```python
import jax
import jax.numpy as jnp
from jax import lax
from jax.sharding import PartitionSpec as P

MOST = 96
BF16 = jnp.bfloat16
F32 = jnp.float32


def dot(lhs, rhs, lhs_dim, rhs_dim):
    return lax.dot_general(lhs, rhs, (((lhs_dim,), (rhs_dim,)), ((), ())), preferred_element_type=F32)


def after(value, *others):
    return lax.optimization_barrier((value, others))[0]


def body(tokens, labels, grad_out, w_gate, w_up, w_down):
    local = w_gate.shape[0]
    groups = lax.axis_size("expert")
    cores = lax.axis_size("tensor")
    peers = lax.axis_size("dp")
    experts = local * groups
    rows = groups * MOST
    half, quarter = rows // 2, rows // 4
    share = MOST // cores
    part = MOST // 4
    paired = cores == 2
    me = lax.axis_index("dp")
    group = lax.axis_index("expert")
    core = lax.axis_index("tensor")

    def over_dp(value, bit):
        return lax.ppermute(value, "dp", [(i, i ^ bit) for i in range(peers)])

    def over_groups(value, shift):
        return lax.ppermute(value, "expert", [(i, (i + shift) % groups) for i in range(groups)])

    def other_core(value):
        return lax.ppermute(value, "tensor", [(0, 1), (1, 0)])

    first = [1 + j % 2 for j in range(local)]
    second = [2 - j % 2 for j in range(local)]

    domain = labels[:, 0]
    onehot = domain[:, None] == jnp.arange(experts, dtype=jnp.int32)[None, :]
    count = domain.shape[0]
    ahead = (jnp.arange(count)[:, None] > jnp.arange(count)[None, :]).astype(BF16)
    before = dot(ahead, onehot.astype(BF16), 1, 0)
    rank_in = jnp.sum(jnp.where(onehot, before, 0.0), axis=1).astype(jnp.int32)
    slot_of = rank_in * experts + domain

    def slots_held(of_core):
        place = jnp.arange(share, dtype=jnp.int32)[None, None, :]
        if not paired:
            place = place + of_core * share
        expert_in = jnp.arange(local, dtype=jnp.int32)[None, :, None]
        to_group = (group + jnp.arange(groups, dtype=jnp.int32)[:, None, None]) % groups
        bit_first = 1 + expert_in % 2
        bit_second = 2 - expert_in % 2
        position = place // part
        owner = (position // 2) * bit_first + (position % 2) * bit_second
        owner = owner ^ me
        if paired:
            owner = owner ^ (of_core * bit_first)
        rank = owner * part + place % part
        return (rank * experts + to_group * local + expert_in).reshape(-1)

    own_slots = slots_held(core)
    to_slots = (own_slots[:, None] == slot_of[None, :]).astype(BF16)

    def send_out(value):
        packed = dot(to_slots, value, 1, 0).astype(BF16).reshape(groups, local, share, -1)
        return [packed[0]] + [over_groups(packed[k], k) for k in range(1, groups)]

    def take_in(arrived):
        mine = jnp.stack(arrived)
        if paired:
            both = jnp.stack([mine, other_core(mine)])
        else:
            both = lax.all_gather(mine, "tensor", axis=0, tiled=False)
        inner = min(share, part)
        both = both.reshape(cores, groups, local, share // inner, inner, -1)
        both = both.transpose(2, 0, 3, 1, 4, 5).reshape(local, rows, -1)
        return [both[j] for j in range(local)]

    def send_half(source, weight, dim):
        return [dot(source[j][half:], weight[j], 1, dim).astype(BF16) for j in range(local)]

    def keep_half(source, weight, dim):
        return [dot(source[j][:half], weight[j], 1, dim) for j in range(local)]

    def step_one(sent):
        return [over_dp(sent[j], first[j]) for j in range(local)]

    def step_two(kept, got):
        sums = []
        for j in range(local):
            passed = (kept[j][quarter:] + got[j][quarter:].astype(F32)).astype(BF16)
            last = over_dp(passed, second[j])
            sums.append(kept[j][:quarter] + got[j][:quarter].astype(F32) + last.astype(F32))
        return sums

    def gather_rows(owned):
        full = []
        for j in range(local):
            a = owned[j]
            b = over_dp(a, second[j])
            c = over_dp(a, first[j])
            d = over_dp(b, first[j])
            full.append((a, b, c, d))
        return full

    def joined(pieces):
        return [jnp.concatenate(p, axis=0) for p in pieces]

    def share_rows(value):
        stacked = jnp.stack(value)
        width = stacked.shape[-1]
        if paired:
            summed = stacked[:, :half] + other_core(stacked[:, half:])
        else:
            summed = lax.psum_scatter(stacked, "tensor", scatter_dimension=1, tiled=True)
        inner = min(share, part)
        summed = summed.astype(BF16).reshape(local, share // inner, groups, inner, width)
        blocks = summed.transpose(2, 0, 1, 3, 4).reshape(groups, local, share, width)
        home = [blocks[0]] + [over_groups(blocks[k], -k) for k in range(1, groups)]
        return jnp.stack(home).reshape(groups * local * share, width)

    def to_tokens(home):
        if paired:
            every = jnp.concatenate([home, other_core(home)], axis=0)
            held = jnp.concatenate([own_slots, slots_held(1 - core)])
        else:
            every = lax.all_gather(home, "tensor", axis=0, tiled=True)
            held = jnp.concatenate([slots_held(c) for c in range(cores)])
        from_slots = (slot_of[:, None] == held[None, :]).astype(BF16)
        return dot(from_slots, every, 1, 0).astype(BF16)

    inputs = take_in(send_out(tokens))
    gate_sent = send_half(inputs, w_gate, 0)
    gate_got = step_one(gate_sent)
    grads_out = send_out(after(grad_out, inputs))
    up_sent = send_half(inputs, w_up, 0)
    up_got = step_one(up_sent)
    gate_kept = keep_half(after(inputs, up_sent), w_gate, 0)
    grad_rows = take_in(after(grads_out, gate_kept))
    up_kept = keep_half(inputs, w_up, 0)
    back_sent = send_half(grad_rows, w_down, 1)
    back_got = step_one(after(back_sent, gate_got))
    gate_sum = step_two(gate_kept, gate_got)
    back_kept = keep_half(grad_rows, w_down, 1)
    up_sum = step_two(up_kept, up_got)

    hidden = []
    for j in range(local):
        hidden.append((gate_sum[j] * jax.nn.sigmoid(gate_sum[j]) * up_sum[j]).astype(BF16))
    hidden_pieces = gather_rows(hidden)
    back_sum = step_two(back_kept, back_got)
    d_gate, d_up = [], []
    for j in range(local):
        g, u, b = gate_sum[j], up_sum[j], back_sum[j]
        s = jax.nn.sigmoid(g)
        d_gate.append((b * u * (s * (1.0 + g * (1.0 - s)))).astype(BF16))
        d_up.append((b * (g * s)).astype(BF16))

    gate_pieces = gather_rows(after(d_gate, [p[2] for p in hidden_pieces]))
    hidden_rows = joined(hidden_pieces)
    forward = [dot(hidden_rows[j], w_down[j], 1, 0) for j in range(local)]
    mixed = to_tokens(share_rows(forward))
    up_pieces = gather_rows(after(d_up, [p[2] for p in gate_pieces]))
    gate_rows = joined(gate_pieces)
    up_rows = joined(up_pieces)
    backward = [dot(gate_rows[j], w_gate[j], 1, 1) + dot(up_rows[j], w_up[j], 1, 1) for j in range(local)]

    def outer(left, right):
        return jnp.einsum(
            "jrd,jrf->jdf", jnp.stack(left), jnp.stack(right), preferred_element_type=F32
        ).astype(BF16)

    grad_down = outer(hidden_rows, grad_rows)
    grad_gate = outer(inputs, after(gate_rows, mixed))
    grad_home = share_rows(backward)
    grad_up = outer(inputs, after(up_rows, backward))
    grad_tokens = to_tokens(grad_home)
    return mixed, grad_tokens, grad_gate, grad_up, grad_down


def solution(mesh):
    in_specs = (
        P("expert", "dp"),
        P("expert", None),
        P("expert", "dp"),
        P("expert", "dp", "tensor"),
        P("expert", "dp", "tensor"),
        P("expert", "tensor", "dp"),
    )
    out_specs = (
        P("expert", "dp"),
        P("expert", "dp"),
        P("expert", "dp", "tensor"),
        P("expert", "dp", "tensor"),
        P("expert", "tensor", "dp"),
    )
    return jax.shard_map(body, mesh=mesh, in_specs=in_specs, out_specs=out_specs, check_vma=False)
```

time: 790 us -> 422 us (0.53)
  waiting for transfers between devices: 491 us -> 196 us
  blocking collectives: 73.3 us -> 0 us
  starting transfers between devices: 5.08 us -> 52.8 us
  other arithmetic: 40.6 us -> 15.9 us
  local copies, waits for them, and re-layouts: 25.6 us -> 9.83 us
  between operations: 14.1 us -> 1.61 us
  matrix products: 132 us -> 140 us
    reduce_scatter x2 -> x0, waiting for transfers between devices: 302 us -> none  [the longest x1 286 us: body(): lax.psum_scatter(jnp.concatenate([gate_part, up_part, back_part], axis=-1...]
    ppermute x0 -> x48, waiting for transfers between devices: none -> 196 us  [the longest x30 156 us: over_dp(): return lax.ppermute(value, 'dp', [(i, i ^ bit) for i in range(peers)])]
    all_gather x2 -> x0, waiting for transfers between devices: 155 us -> none  [the longest x1 155 us: body(): act_rows = lax.all_gather(local_acts, 'dp', axis=0, tiled=True)]
    all_to_all x1 -> x0, blocking collectives: 73.3 us -> none  [body(): lax.all_to_all(packed, 'expert', split_axis=1, concat_axis=1, tiled=True)]
    ppermute x0 -> x48, starting transfers between devices: none -> 52.8 us  [the longest x30 20.8 us: over_dp(): return lax.ppermute(value, 'dp', [(i, i ^ bit) for i in range(peers)])]
    all_to_all x1 -> x0, waiting for transfers between devices: 33.4 us -> none  [body(): lax.all_to_all(shares_part, 'expert', split_axis=1, concat_axis=1, tiled=...]
    concatenate x3 -> x1, other arithmetic: 31 us -> 0.6 us  [to_tokens(): held = jnp.concatenate([own_slots, slots_held(1 - core)])]
    reshape x3 -> x0, local copies, waits for them, and re-layouts: 15.5 us -> none  [the longest x2 9.77 us: body(): packed = packed.reshape(MOST, groups, local_experts, 2 * feat_width)]
  transfers between devices with their start and end apart: 5 -> 48, of which waited for: 4 -> 21; matrix products, arithmetic and copies ran while one was open for 5% -> 35% of each run, Pallas kernels for 0% -> 0%
where the time goes in v1:
time: 422 us; the launch traced here: 416 us
  waiting for transfers between devices  196 us (46%)
  matrix products  140 us (33%)
  starting transfers between devices  52.8 us (13%)
  other arithmetic  15.9 us (4%)
  local copies, waits for them, and re-layouts  9.83 us (2%)
    ppermute x30, waiting for transfers between devices, over_dp(): return lax.ppermute(value, 'dp', [(i, i ^ bit) for i in range(peers)])  156 us
    dot_general x23, matrix products, dot(): lax.dot_general(lhs, rhs, (((lhs_dim,), (rhs_dim,)), ((), ())), preferred...  102 us
    dot_general x3, matrix products, outer(): jnp.einsum('jrd,jrf->jdf', jnp.stack(left), jnp.stack(right), preferred_e...  38 us
    ppermute x12, waiting for transfers between devices, over_groups(): lax.ppermute(value, 'expert', [(i, (i + shift) % groups) for i in range(g...  37.4 us
    ppermute x30, starting transfers between devices, over_dp(): return lax.ppermute(value, 'dp', [(i, i ^ bit) for i in range(peers)])  20.8 us
    ppermute x6, starting transfers between devices, other_core(): return lax.ppermute(value, 'tensor', [(0, 1), (1, 0)])  16.2 us
    ppermute x12, starting transfers between devices, over_groups(): lax.ppermute(value, 'expert', [(i, (i + shift) % groups) for i in range(g...  15.8 us
  transfers between devices with their start and end apart: 48, of which 21 were waited for; matrix products, arithmetic and copies ran while one was open for 35% of the time, Pallas kernels for 0%

profile of v1, /device:TPU:11, one launch (start us, length us, event | category | flops | bytes accessed | tf_op | source)
XLA Modules:
  0.0 416.2 jit_solution(1764671327016335081)
XLA Ops:
  7.2 11.5 %collective-permute-done.1 = bf16[2,48,1024]{2,1,0:T(8,128)(2,1)S(1)} collective-permute-done((bf16[2,48,1024]{2,1,0:T(8,128)(2,1)S(1)}, bf16[2,48,1024]{2,1,0:T(8,128)(2,1)S(1)}, u32[]{:S(2)}, u32[]{:S(2)}) %collective-permute-start.1) | collective-permute-done | bytes 196640 | tf_op jit(solution)/shard_map/ppermute | solution.py:38
  56.2 6.2 %collective-permute-done.25 = bf16[2,48,1024]{2,1,0:T(8,128)(2,1)S(1)} collective-permute-done((bf16[2,48,1024]{2,1,0:T(8,128)(2,1)S(1)}, bf16[2,48,1024]{2,1,0:T(8,128)(2,1)S(1)}, u32[]{:S(2)}, u32[]{:S(2)}) %collective-permute-start.25) | collective-permute-done | bytes 196640 | tf_op jit(solution)/shard_map/ppermute | solution.py:38
  74.5 6.7 %fusion.78 = bf16[192,3584]{1,0:T(8,128)(2,1)} fusion(bf16[192,1024]{1,0:T(8,128)(2,1)S(1)} %bitcast.207, bf16[2,3584,1024]{2,1,0:T(8,128)(2,1)} %param.11), kind=kOutput, calls=%fused_computation.71 | convolution fusion | flops 1409974272 | bytes 9109504 | tf_op jit(solution)/shard_map/dot_general | solution.py:12
  86.9 6.7 %fusion.72 = bf16[192,3584]{1,0:T(8,128)(2,1)} fusion(bf16[192,1024]{1,0:T(8,128)(2,1)S(1)} %bitcast.205, bf16[2,3584,1024]{2,1,0:T(8,128)(2,1)} %param.11), kind=kOutput, calls=%fused_computation.69 | convolution fusion | flops 1409974272 | bytes 9109504 | tf_op jit(solution)/shard_map/dot_general | solution.py:12
  93.7 6.1 %fusion.14 = f32[192,3584]{1,0:T(8,128)S(1)} fusion(bf16[192,1024]{1,0:T(8,128)(2,1)S(1)} %bitcast.204, bf16[2,3584,1024]{2,1,0:T(8,128)(2,1)} %param.11), kind=kOutput, calls=%fused_computation.17 | convolution fusion | flops 1409286144 | bytes 10485760 | tf_op jit(solution)/shard_map/dot_general | solution.py:12
  106.0 41.2 %collective-permute-done.29 = bf16[192,3584]{1,0:T(8,128)(2,1)S(1)} collective-permute-done((bf16[192,3584]{1,0:T(8,128)(2,1)S(1)}, bf16[192,3584]{1,0:T(8,128)(2,1)S(1)}, u32[]{:S(2)}, u32[]{:S(2)}) %collective-permute-start.29) | collective-permute-done | bytes 1376288 | tf_op jit(solution)/shard_map/ppermute | solution.py:35
  149.4 10.3 %collective-permute-done.12 = bf16[96,3584]{1,0:T(8,128)(2,1)} collective-permute-done((bf16[96,3584]{1,0:T(8,128)(2,1)S(1)}, bf16[96,3584]{1,0:T(8,128)(2,1)}, u32[]{:S(2)}, u32[]{:S(2)}) %collective-permute-start.12) | collective-permute-done | bytes 688160 | tf_op jit(solution)/shard_map/ppermute | solution.py:35
  159.6 14.7 %collective-permute-done.30 = bf16[96,3584]{1,0:T(8,128)(2,1)} collective-permute-done((bf16[96,3584]{1,0:T(8,128)(2,1)S(1)}, bf16[96,3584]{1,0:T(8,128)(2,1)}, u32[]{:S(2)}, u32[]{:S(2)}) %collective-permute-start.30) | collective-permute-done | bytes 688160 | tf_op jit(solution)/shard_map/ppermute | solution.py:35
  196.6 12.8 %collective-permute-done.15 = bf16[96,3584]{1,0:T(8,128)(2,1)} collective-permute-done((bf16[96,3584]{1,0:T(8,128)(2,1)}, bf16[96,3584]{1,0:T(8,128)(2,1)}, u32[]{:S(2)}, u32[]{:S(2)}) %collective-permute-start.15) | collective-permute-done | bytes 688160 | tf_op jit(solution)/shard_map/ppermute | solution.py:35
  210.0 14.0 %collective-permute-done.32 = bf16[96,3584]{1,0:T(8,128)(2,1)S(1)} collective-permute-done((bf16[96,3584]{1,0:T(8,128)(2,1)S(1)}, bf16[96,3584]{1,0:T(8,128)(2,1)S(1)}, u32[]{:S(2)}, u32[]{:S(2)}) %collective-permute-start.32) | collective-permute-done | bytes 688160 | tf_op jit(solution)/shard_map/ppermute | solution.py:35
  224.5 11.5 %collective-permute-done.34 = bf16[96,3584]{1,0:T(8,128)(2,1)S(1)} collective-permute-done((bf16[96,3584]{1,0:T(8,128)(2,1)S(1)}, bf16[96,3584]{1,0:T(8,128)(2,1)S(1)}, u32[]{:S(2)}, u32[]{:S(2)}) %collective-permute-start.34) | collective-permute-done | bytes 688160 | tf_op jit(solution)/shard_map/ppermute | solution.py:35
  236.3 14.4 %collective-permute-done.17 = bf16[96,3584]{1,0:T(8,128)(2,1)S(1)} collective-permute-done((bf16[96,3584]{1,0:T(8,128)(2,1)}, bf16[96,3584]{1,0:T(8,128)(2,1)S(1)}, u32[]{:S(2)}, u32[]{:S(2)}) %collective-permute-start.17) | collective-permute-done | bytes 688160 | tf_op jit(solution)/shard_map/ppermute | solution.py:35
  251.4 6.7 %fusion.113 = f32[1,384,1024]{2,1,0:T(8,128)S(1)} fusion(bf16[2,3584,1024]{2,1,0:T(8,128)(2,1)} %param.11, bf16[96,3584]{1,0:T(8,128)(2,1)S(1)} %collective-permute-done.17, bf16[96,3584]{1,0:T(8,128)(2,1)} %collective-permute-done.16, bf16[96,3584]{1,0:T(8,128)(2,1)} %collective-permute-done.15, bf16[96,3584]{1,0:T(8,128)(2,1)} %get-tuple-element.41), kind=kOutput, calls=%fused_computation.105 | convolution fusion | flops 2829582336 | bytes 11665408 | tf_op jit(solution)/shard_map/dot_general | solution.py:12
  259.8 6.5 %fusion.110 = f32[1,384,1024]{2,1,0:T(8,128)S(1)} fusion(bf16[2,3584,1024]{2,1,0:T(8,128)(2,1)} %param.11, bf16[96,3584]{1,0:T(8,128)(2,1)S(1)} %collective-permute-done.10, bf16[96,3584]{1,0:T(8,128)(2,1)} %collective-permute-done.9, bf16[96,3584]{1,0:T(8,128)(2,1)S(1)} %collective-permute-done.8, bf16[96,3584]{1,0:T(8,128)(2,1)} %get-tuple-element.44), kind=kOutput, calls=%fused_computation.104 | convolution fusion | flops 2829582336 | bytes 11665408 | tf_op jit(solution)/shard_map/dot_general | solution.py:12
  270.2 7.8 %collective-permute-start.18 = (f32[2,192,1024]{2,1,0:T(8,128)S(1)}, f32[2,192,1024]{2,1,0:T(8,128)S(1)}, u32[]{:S(2)}, u32[]{:S(2)}) collective-permute-start(f32[2,192,1024]{2,1,0:T(8,128)S(1)} %pad_maximum_fusion.3), channel_id=1, source_target_pairs={{0,1},{1,0},{2,3},{3,2},{4,5},{5,4},{6,7},{7,6},{8,9},{9,8},{10,11... | collective-permute-start | bytes 4718600 | tf_op jit(solution)/shard_map/ppermute | solution.py:41
  284.1 14.1 %collective-permute-done.33 = bf16[96,3584]{1,0:T(8,128)(2,1)S(1)} collective-permute-done((bf16[96,3584]{1,0:T(8,128)(2,1)S(1)}, bf16[96,3584]{1,0:T(8,128)(2,1)S(1)}, u32[]{:S(2)}, u32[]{:S(2)}) %collective-permute-start.33) | collective-permute-done | bytes 688160 | tf_op jit(solution)/shard_map/ppermute | solution.py:35
  298.3 14.6 %collective-permute-done.37 = bf16[96,3584]{1,0:T(8,128)(2,1)S(1)} collective-permute-done((bf16[96,3584]{1,0:T(8,128)(2,1)S(1)}, bf16[96,3584]{1,0:T(8,128)(2,1)S(1)}, u32[]{:S(2)}, u32[]{:S(2)}) %collective-permute-start.37) | collective-permute-done | bytes 688160 | tf_op jit(solution)/shard_map/ppermute | solution.py:35
  313.8 6.2 %fusion.30 = f32[384,1024]{1,0:T(8,128)S(1)} fusion(bf16[384,3584]{1,0:T(8,128)(2,1)} %constant_dynamic-update-slice_fusion.4, bf16[2,1024,3584]{2,1,0:T(8,128)(2,1)} %param.10), kind=kOutput, calls=%fused_computation.33 | convolution fusion | flops 2818572288 | bytes 11665408 | tf_op jit(solution)/shard_map/dot_general | solution.py:12
  320.0 6.2 %fusion.116 = f32[384,1024]{1,0:T(8,128)S(1)} fusion(f32[384,1024]{1,0:T(8,128)S(1)} %fusion.30, bf16[384,3584]{1,0:T(8,128)(2,1)} %copy-done.13, bf16[2,1024,3584]{2,1,0:T(8,128)(2,1)} %param.9), kind=kOutput, calls=%fused_computation.106 | convolution fusion | flops 2818965504 | bytes 13238272 | tf_op jit(solution)/shard_map/dot_general | solution.py:12
  326.2 6.3 %fusion.24 = f32[384,1024]{1,0:T(8,128)S(1)} fusion(bf16[384,3584]{1,0:T(8,128)(2,1)S(1)} %constant_dynamic-update-slice_fusion.12, bf16[2,1024,3584]{2,1,0:T(8,128)(2,1)} %param.10), kind=kOutput, calls=%fused_computation.27 | convolution fusion | flops 2818572288 | bytes 11665408 | tf_op jit(solution)/shard_map/dot_general | solution.py:12
  348.8 12.7 %convolution_convert_fusion = bf16[2,3584,1024]{2,1,0:T(8,128)(2,1)} fusion(bf16[1,384,3584]{2,1,0:T(8,128)(2,1)S(1)} %fusion.143, bf16[1,384,3584]{2,1,0:T(8,128)(2,1)S(1)} %fusion.144, bf16[1,384,1024]{2,1,0:T(8,128)(2,1)} %bitcast.201, bf16[1,384,1024]{2,1,0:T(8,128)(2,1)} %bitcast.200), kind=kOutput, calls=%fused_computation | convolution fusion | flops 5648023552 | bytes 21757952 | tf_op jit(solution)/shard_map/jrd,jrf->jdf/dot_general | solution.py:178
  366.4 13.6 %convolution_convert_fusion.1 = bf16[2,1024,3584]{2,1,0:T(8,128)(2,1)} fusion(bf16[1,384,3584]{2,1,0:T(8,128)(2,1)} %bitcast.232, bf16[1,384,3584]{2,1,0:T(8,128)(2,1)} %bitcast.80, bf16[1,384,1024]{1,2,0:T(8,128)(2,1)S(1)} %copy-done.6, bf16[1,384,1024]{1,2,0:T(8,128)(2,1)S(1)} %copy-done.8), kind=kOutput, calls=%fused_computation.1 | convolution fusion | flops 5648023552 | bytes 21757952 | tf_op jit(solution)/shard_map/jrd,jrf->jdf/dot_general | solution.py:178
  389.3 8.4 %collective-permute-done.45 = bf16[2,48,1024]{2,1,0:T(8,128)(2,1)S(1)} collective-permute-done((bf16[2,48,1024]{2,1,0:T(8,128)(2,1)S(1)}, bf16[2,48,1024]{2,1,0:T(8,128)(2,1)S(1)}, u32[]{:S(2)}, u32[]{:S(2)}) %collective-permute-start.45) | collective-permute-done | bytes 196640 | tf_op jit(solution)/shard_map/ppermute | solution.py:38
  402.3 11.6 %convolution_convert_fusion.2 = bf16[2,1024,3584]{2,1,0:T(8,128)(2,1)} fusion(bf16[1,384,3584]{2,1,0:T(8,128)(2,1)S(1)} %bitcast.231, bf16[1,384,3584]{2,1,0:T(8,128)(2,1)S(1)} %bitcast.233, bf16[1,384,1024]{1,2,0:T(8,128)(2,1)S(1)} %copy-done.7, bf16[1,384,1024]{1,2,0:T(8,128)(2,1)S(1)} %copy-done.9), kind=kOutput, calls=%fused_computation.2 | convolution fusion | flops 5648023552 | bytes 21757952 | tf_op jit(solution)/shard_map/jrd,jrf->jdf/dot_general | solution.py:178
  (208 shorter events, 143.6 us)
Async XLA Ops:
  40.0 62.5 %collective-permute-start.13 = (bf16[192,3584]{1,0:T(8,128)(2,1)S(1)}, bf16[192,3584]{1,0:T(8,128)(2,1)S(1)}, u32[]{:S(2)}, u32[]{:S(2)}) collective-permute-start(bf16[192,3584]{1,0:T(8,128)(2,1)S(1)} %fusion.66), channel_id=1, source_target_pairs={{0,16},{8,24},{16,0},{24,8},{1,17},{9,25},{17,1},{25,9},{2,18},{10... | collective-permute-start | bytes 4128776 | tf_op jit(solution)/shard_map/ppermute | solution.py:35
  41.3 62.9 %collective-permute-start.6 = (bf16[192,3584]{1,0:T(8,128)(2,1)}, bf16[192,3584]{1,0:T(8,128)(2,1)S(1)}, u32[]{:S(2)}, u32[]{:S(2)}) collective-permute-start(bf16[192,3584]{1,0:T(8,128)(2,1)} %fusion.63), channel_id=1, source_target_pairs={{0,8},{8,0},{16,24},{24,16},{1,9},{9,1},{17,25},{25,17},{2,10},{10... | collective-permute-start | bytes 4128776 | tf_op jit(solution)/shard_map/ppermute | solution.py:35
  55.4 47.6 %collective-permute-start.11 = (bf16[192,3584]{1,0:T(8,128)(2,1)S(1)}, bf16[192,3584]{1,0:T(8,128)(2,1)S(1)}, u32[]{:S(2)}, u32[]{:S(2)}) collective-permute-start(bf16[192,3584]{1,0:T(8,128)(2,1)S(1)} %fusion.75), channel_id=1, source_target_pairs={{0,16},{8,24},{16,0},{24,8},{1,17},{9,25},{17,1},{25,9},{2,18},{10... | collective-permute-start | bytes 4128776 | tf_op jit(solution)/shard_map/ppermute | solution.py:35
  62.4 39.6 %collective-permute-start.4 = (bf16[192,3584]{1,0:T(8,128)(2,1)S(1)}, bf16[192,3584]{1,0:T(8,128)(2,1)S(1)}, u32[]{:S(2)}, u32[]{:S(2)}) collective-permute-start(bf16[192,3584]{1,0:T(8,128)(2,1)S(1)} %fusion.69), channel_id=1, source_target_pairs={{0,8},{8,0},{16,24},{24,16},{1,9},{9,1},{17,25},{25,17},{2,10},{10... | collective-permute-start | bytes 4128776 | tf_op jit(solution)/shard_map/ppermute | solution.py:35
  102.2 77.7 %collective-permute-start.5 = (bf16[96,3584]{1,0:T(8,128)(2,1)S(1)}, bf16[96,3584]{1,0:T(8,128)(2,1)S(1)}, u32[]{:S(2)}, u32[]{:S(2)}) collective-permute-start(bf16[96,3584]{1,0:T(8,128)(2,1)S(1)} %fusion.132), channel_id=1, source_target_pairs={{0,16},{8,24},{16,0},{24,8},{1,17},{9,25},{17,1},{25,9},{2,18},{10... | collective-permute-start | bytes 2064392 | tf_op jit(solution)/shard_map/ppermute | solution.py:35
  102.7 46.3 %collective-permute-start.14 = (bf16[96,3584]{1,0:T(8,128)(2,1)S(1)}, bf16[96,3584]{1,0:T(8,128)(2,1)S(1)}, u32[]{:S(2)}, u32[]{:S(2)}) collective-permute-start(bf16[96,3584]{1,0:T(8,128)(2,1)S(1)} %fusion.126), channel_id=1, source_target_pairs={{0,8},{8,0},{16,24},{24,16},{1,9},{9,1},{17,25},{25,17},{2,10},{10... | collective-permute-start | bytes 2064392 | tf_op jit(solution)/shard_map/ppermute | solution.py:35
  103.0 44.1 %collective-permute-start.29 = (bf16[192,3584]{1,0:T(8,128)(2,1)S(1)}, bf16[192,3584]{1,0:T(8,128)(2,1)S(1)}, u32[]{:S(2)}, u32[]{:S(2)}) collective-permute-start(bf16[192,3584]{1,0:T(8,128)(2,1)S(1)} %copy-done.20), channel_id=1, source_target_pairs={{0,16},{8,24},{16,0},{24,8},{1,17},{9,25},{17,1},{25,9},{2,18},{10... | collective-permute-start | bytes 4128776 | tf_op jit(solution)/shard_map/ppermute | solution.py:35
  104.4 75.6 %collective-permute-start.7 = (bf16[96,3584]{1,0:T(8,128)(2,1)S(1)}, bf16[96,3584]{1,0:T(8,128)(2,1)S(1)}, u32[]{:S(2)}, u32[]{:S(2)}) collective-permute-start(bf16[96,3584]{1,0:T(8,128)(2,1)S(1)} %fusion.130), channel_id=1, source_target_pairs={{0,16},{8,24},{16,0},{24,8},{1,17},{9,25},{17,1},{25,9},{2,18},{10... | collective-permute-start | bytes 2064392 | tf_op jit(solution)/shard_map/ppermute | solution.py:35
  104.7 43.0 %collective-permute-start.27 = (bf16[192,3584]{1,0:T(8,128)(2,1)S(1)}, bf16[192,3584]{1,0:T(8,128)(2,1)S(1)}, u32[]{:S(2)}, u32[]{:S(2)}) collective-permute-start(bf16[192,3584]{1,0:T(8,128)(2,1)S(1)} %copy-done.19), channel_id=1, source_target_pairs={{0,8},{8,0},{16,24},{24,16},{1,9},{9,1},{17,25},{25,17},{2,10},{10... | collective-permute-start | bytes 4128776 | tf_op jit(solution)/shard_map/ppermute | solution.py:35
  147.6 26.7 %collective-permute-start.30 = (bf16[96,3584]{1,0:T(8,128)(2,1)S(1)}, bf16[96,3584]{1,0:T(8,128)(2,1)}, u32[]{:S(2)}, u32[]{:S(2)}) collective-permute-start(bf16[96,3584]{1,0:T(8,128)(2,1)S(1)} %fusion.122), channel_id=1, source_target_pairs={{0,8},{8,0},{16,24},{24,16},{1,9},{9,1},{17,25},{25,17},{2,10},{10... | collective-permute-start | bytes 2064392 | tf_op jit(solution)/shard_map/ppermute | solution.py:35
  149.0 31.0 %collective-permute-start.28 = (bf16[96,3584]{1,0:T(8,128)(2,1)S(1)}, bf16[96,3584]{1,0:T(8,128)(2,1)S(1)}, u32[]{:S(2)}, u32[]{:S(2)}) collective-permute-start(bf16[96,3584]{1,0:T(8,128)(2,1)S(1)} %fusion.124), channel_id=1, source_target_pairs={{0,16},{8,24},{16,0},{24,8},{1,17},{9,25},{17,1},{25,9},{2,18},{10... | collective-permute-start | bytes 2064392 | tf_op jit(solution)/shard_map/ppermute | solution.py:35
  182.8 26.6 %collective-permute-start.15 = (bf16[96,3584]{1,0:T(8,128)(2,1)}, bf16[96,3584]{1,0:T(8,128)(2,1)}, u32[]{:S(2)}, u32[]{:S(2)}) collective-permute-start(bf16[96,3584]{1,0:T(8,128)(2,1)} %get-tuple-element.41), channel_id=1, source_target_pairs={{0,8},{8,0},{16,24},{24,16},{1,9},{9,1},{17,25},{25,17},{2,10},{10... | collective-permute-start | bytes 2064392 | tf_op jit(solution)/shard_map/ppermute | solution.py:35
  194.7 29.4 %collective-permute-start.32 = (bf16[96,3584]{1,0:T(8,128)(2,1)S(1)}, bf16[96,3584]{1,0:T(8,128)(2,1)S(1)}, u32[]{:S(2)}, u32[]{:S(2)}) collective-permute-start(bf16[96,3584]{1,0:T(8,128)(2,1)S(1)} %copy-done.5), channel_id=1, source_target_pairs={{0,8},{8,0},{16,24},{24,16},{1,9},{9,1},{17,25},{25,17},{2,10},{10... | collective-permute-start | bytes 2064392 | tf_op jit(solution)/shard_map/ppermute | solution.py:35
  195.1 72.9 %collective-permute-start.31 = (bf16[96,3584]{1,0:T(8,128)(2,1)S(1)}, bf16[96,3584]{1,0:T(8,128)(2,1)S(1)}, u32[]{:S(2)}, u32[]{:S(2)}) collective-permute-start(bf16[96,3584]{1,0:T(8,128)(2,1)S(1)} %copy-done.5), channel_id=1, source_target_pairs={{0,16},{8,24},{16,0},{24,8},{1,17},{9,25},{17,1},{25,9},{2,18},{10... | collective-permute-start | bytes 2064392 | tf_op jit(solution)/shard_map/ppermute | solution.py:35
  195.1 40.8 %collective-permute-start.34 = (bf16[96,3584]{1,0:T(8,128)(2,1)S(1)}, bf16[96,3584]{1,0:T(8,128)(2,1)S(1)}, u32[]{:S(2)}, u32[]{:S(2)}) collective-permute-start(bf16[96,3584]{1,0:T(8,128)(2,1)S(1)} %copy-done.3), channel_id=1, source_target_pairs={{0,16},{8,24},{16,0},{24,8},{1,17},{9,25},{17,1},{25,9},{2,18},{10... | collective-permute-start | bytes 2064392 | tf_op jit(solution)/shard_map/ppermute | solution.py:35
  209.4 41.3 %collective-permute-start.17 = (bf16[96,3584]{1,0:T(8,128)(2,1)}, bf16[96,3584]{1,0:T(8,128)(2,1)S(1)}, u32[]{:S(2)}, u32[]{:S(2)}) collective-permute-start(bf16[96,3584]{1,0:T(8,128)(2,1)} %collective-permute-done.15), channel_id=1, source_target_pairs={{0,16},{8,24},{16,0},{24,8},{1,17},{9,25},{17,1},{25,9},{2,18},{10... | collective-permute-start | bytes 2064392 | tf_op jit(solution)/shard_map/ppermute | solution.py:35
  209.5 60.6 %collective-permute-start.38 = (bf16[96,3584]{1,0:T(8,128)(2,1)S(1)}, bf16[96,3584]{1,0:T(8,128)(2,1)S(1)}, u32[]{:S(2)}, u32[]{:S(2)}) collective-permute-start(bf16[96,3584]{1,0:T(8,128)(2,1)S(1)} %copy-done.3), channel_id=1, source_target_pairs={{0,8},{8,0},{16,24},{24,16},{1,9},{9,1},{17,25},{25,17},{2,10},{10... | collective-permute-start | bytes 2064392 | tf_op jit(solution)/shard_map/ppermute | solution.py:35
  224.1 35.0 %collective-permute-start.10 = (bf16[96,3584]{1,0:T(8,128)(2,1)S(1)}, bf16[96,3584]{1,0:T(8,128)(2,1)S(1)}, u32[]{:S(2)}, u32[]{:S(2)}) collective-permute-start(bf16[96,3584]{1,0:T(8,128)(2,1)S(1)} %collective-permute-done.8), channel_id=1, source_target_pairs={{0,8},{8,0},{16,24},{24,16},{1,9},{9,1},{17,25},{25,17},{2,10},{10... | collective-permute-start | bytes 2064392 | tf_op jit(solution)/shard_map/ppermute | solution.py:35
  236.0 44.3 %collective-permute-start.36 = (bf16[96,3584]{1,0:T(8,128)(2,1)S(1)}, bf16[96,3584]{1,0:T(8,128)(2,1)S(1)}, u32[]{:S(2)}, u32[]{:S(2)}) collective-permute-start(bf16[96,3584]{1,0:T(8,128)(2,1)S(1)} %copy-done.4), channel_id=1, source_target_pairs={{0,8},{8,0},{16,24},{24,16},{1,9},{9,1},{17,25},{25,17},{2,10},{10... | collective-permute-start | bytes 2064392 | tf_op jit(solution)/shard_map/ppermute | solution.py:35
  250.7 27.4 %collective-permute-start.35 = (bf16[96,3584]{1,0:T(8,128)(2,1)S(1)}, bf16[96,3584]{1,0:T(8,128)(2,1)S(1)}, u32[]{:S(2)}, u32[]{:S(2)}) collective-permute-start(bf16[96,3584]{1,0:T(8,128)(2,1)S(1)} %copy-done.4), channel_id=1, source_target_pairs={{0,16},{8,24},{16,0},{24,8},{1,17},{9,25},{17,1},{25,9},{2,18},{10... | collective-permute-start | bytes 2064392 | tf_op jit(solution)/shard_map/ppermute | solution.py:35
  270.2 74.5 %collective-permute-start.18 = (f32[2,192,1024]{2,1,0:T(8,128)S(1)}, f32[2,192,1024]{2,1,0:T(8,128)S(1)}, u32[]{:S(2)}, u32[]{:S(2)}) collective-permute-start(f32[2,192,1024]{2,1,0:T(8,128)S(1)} %pad_maximum_fusion.3), channel_id=1, source_target_pairs={{0,1},{1,0},{2,3},{3,2},{4,5},{5,4},{6,7},{7,6},{8,9},{9,8},{10,11... | collective-permute-start | bytes 4718600 | tf_op jit(solution)/shard_map/ppermute | solution.py:41
  283.4 29.5 %collective-permute-start.37 = (bf16[96,3584]{1,0:T(8,128)(2,1)S(1)}, bf16[96,3584]{1,0:T(8,128)(2,1)S(1)}, u32[]{:S(2)}, u32[]{:S(2)}) collective-permute-start(bf16[96,3584]{1,0:T(8,128)(2,1)S(1)} %collective-permute-done.35), channel_id=1, source_target_pairs={{0,8},{8,0},{16,24},{24,16},{1,9},{9,1},{17,25},{25,17},{2,10},{10... | collective-permute-start | bytes 2064392 | tf_op jit(solution)/shard_map/ppermute | solution.py:35
  283.9 42.2 %collective-permute-start.42 = (bf16[96,3584]{1,0:T(8,128)(2,1)S(1)}, bf16[96,3584]{1,0:T(8,128)(2,1)S(1)}, u32[]{:S(2)}, u32[]{:S(2)}) collective-permute-start(bf16[96,3584]{1,0:T(8,128)(2,1)S(1)} %collective-permute-done.40), channel_id=1, source_target_pairs={{0,16},{8,24},{16,0},{24,8},{1,17},{9,25},{17,1},{25,9},{2,18},{10... | collective-permute-start | bytes 2064392 | tf_op jit(solution)/shard_map/ppermute | solution.py:35
  339.2 40.8 %collective-permute-start.43 = (f32[2,192,1024]{2,1,0:T(8,128)}, f32[2,192,1024]{2,1,0:T(8,128)S(1)}, u32[]{:S(2)}, u32[]{:S(2)}) collective-permute-start(f32[2,192,1024]{2,1,0:T(8,128)} %pad_maximum_fusion.2), channel_id=1, source_target_pairs={{0,1},{1,0},{2,3},{3,2},{4,5},{5,4},{6,7},{7,6},{8,9},{9,8},{10,11... | collective-permute-start | bytes 4718600 | tf_op jit(solution)/shard_map/ppermute | solution.py:41
  (47 other events, 684.4 us)

commit v2 on v1

--- a/solution.py
+++ b/solution.py
@@ -1,6 +1,8 @@
 import jax
 import jax.numpy as jnp
 from jax import lax
+from jax.experimental import pallas as pl
+from jax.experimental.pallas import tpu as pltpu
 from jax.sharding import PartitionSpec as P
 
 MOST = 96
@@ -12,8 +14,142 @@
     return lax.dot_general(lhs, rhs, (((lhs_dim,), (rhs_dim,)), ((), ())), preferred_element_type=F32)
 
 
-def after(value, *others):
-    return lax.optimization_barrier((value, others))[0]
+VMEM = 56 * 1024 * 1024
+
+
+def kernel_params(flops, moved):
+    return dict(
+        compiler_params=pltpu.CompilerParams(vmem_limit_bytes=VMEM),
+        cost_estimate=pl.CostEstimate(flops=flops, bytes_accessed=moved, transcendentals=0),
+    )
+
+
+def unread(values):
+    return [pl.BlockSpec(memory_space=pl.ANY)] * len(values)
+
+
+def tile_of(width):
+    return width // 2 if width % 256 == 0 else width
+
+
+def back_to_rows(pieces, weight, j, dim, added=(), waits=()):
+    width = pieces[0].shape[1]
+    sizes = [p.shape[0] for p in pieces]
+    rows = sum(sizes)
+    half = rows // 2
+    feat = weight.shape[2 - dim]
+    tile = tile_of(width)
+    count = len(pieces)
+
+    def kernel(*refs):
+        parts, w_ref, start = refs[:count], refs[count], refs[count + 1 : count + 1 + len(added)]
+        low_ref, high_ref = refs[-2:]
+
+        @pl.when(pl.program_id(0) == 0)
+        def _():
+            low_ref[...] = start[0][...] if start else jnp.zeros_like(low_ref)
+            high_ref[...] = start[1][...] if start else jnp.zeros_like(high_ref)
+
+        x = jnp.concatenate([p[...] for p in parts], axis=0)
+        total = dot(x, w_ref[0], 1, dim)
+        low_ref[...] += total[:half]
+        high_ref[...] += total[half:]
+
+    if dim == 0:
+        weight_spec = pl.BlockSpec((1, tile, feat), lambda i: (j, i, 0))
+    else:
+        weight_spec = pl.BlockSpec((1, feat, tile), lambda i: (j, 0, i))
+    whole = pl.BlockSpec((half, feat), lambda i: (0, 0))
+    return pl.pallas_call(
+        kernel,
+        grid=(width // tile,),
+        in_specs=[pl.BlockSpec((n, tile), lambda i: (0, i)) for n in sizes] + [weight_spec] + [whole] * len(added) + unread(waits),
+        out_specs=[whole] * 2,
+        out_shape=[jax.ShapeDtypeStruct((half, feat), F32)] * 2,
+        name="back_to_rows",
+        **kernel_params(2 * rows * feat * width, 2 * feat * width + 2 * rows * width + 4 * rows * feat),
+    )(*pieces, weight, *added, *waits)
+
+
+def outer(x, pieces, shape, j, into, x_first, waits=(), brief=False):
+    width = pieces[0].shape[1]
+    sizes = [p.shape[0] for p in pieces]
+    rows = sum(sizes)
+    feat = x.shape[0] if x_first else x.shape[1]
+    tile = tile_of(width)
+    count = len(pieces)
+
+    def kernel(*refs):
+        x_ref, parts, out_ref = refs[0], refs[1 : 1 + count], refs[-1]
+        y = jnp.concatenate([p[...] for p in parts], axis=0)
+        if x_first:
+            out_ref[0] = dot(x_ref[...], y, 1, 0).astype(BF16)
+        else:
+            out_ref[0] = dot(y, x_ref[...], 0, 0).astype(BF16)
+
+    if x_first:
+        out_spec = pl.BlockSpec((1, feat, tile), lambda i: (j, 0, i))
+    else:
+        out_spec = pl.BlockSpec((1, tile, feat), lambda i: (j, i, 0))
+    return pl.pallas_call(
+        kernel,
+        grid=(width // tile,),
+        in_specs=[pl.BlockSpec(x.shape, lambda i: (0, 0))]
+        + [pl.BlockSpec((n, tile), lambda i: (0, i)) for n in sizes]
+        + unread(into)
+        + unread(waits),
+        out_specs=out_spec,
+        out_shape=jax.ShapeDtypeStruct(shape, BF16),
+        input_output_aliases={1 + count: 0} if into else {},
+        name="outer",
+        **(kernel_params(0, 0) if brief else kernel_params(2 * rows * feat * width, 2 * feat * width + 2 * rows * width)),
+    )(x, *pieces, *into, *waits)
+
+
+def spaced(*values):
+    def kernel(*refs):
+        refs[-1][...] = jnp.zeros_like(refs[-1])
+
+    return pl.pallas_call(
+        kernel,
+        in_specs=unread(values),
+        out_specs=pl.BlockSpec(memory_space=pltpu.VMEM),
+        out_shape=jax.ShapeDtypeStruct((8, 128), F32),
+        name="spaced",
+        cost_estimate=pl.CostEstimate(flops=0, bytes_accessed=1 << 27, transcendentals=0),
+    )(*values)
+
+
+def gathered(values, waits):
+    count = len(values)
+    shape = (count,) + values[0].shape
+
+    def kernel(*refs):
+        for n in range(count):
+            refs[-1][n] = refs[n][...]
+
+    return pl.pallas_call(
+        kernel,
+        in_specs=[pl.BlockSpec(memory_space=pltpu.VMEM)] * count + unread(waits),
+        out_specs=pl.BlockSpec(memory_space=pltpu.VMEM),
+        out_shape=jax.ShapeDtypeStruct(shape, values[0].dtype),
+        name="gathered",
+        **kernel_params(0, 4 * count * values[0].size),
+    )(*values, *waits)
+
+
+def held(value, *waits):
+    def kernel(*refs):
+        refs[-1][...] = refs[0][...]
+
+    return pl.pallas_call(
+        kernel,
+        in_specs=[pl.BlockSpec(memory_space=pltpu.VMEM)] + unread(waits),
+        out_specs=pl.BlockSpec(memory_space=pltpu.VMEM),
+        out_shape=jax.ShapeDtypeStruct(value.shape, value.dtype),
+        name="held",
+        **kernel_params(0, 4 * value.size),
+    )(value, *waits)
 
 
 def body(tokens, labels, grad_out, w_gate, w_up, w_down):
@@ -94,39 +230,46 @@
     def step_one(sent):
         return [over_dp(sent[j], first[j]) for j in range(local)]
 
-    def step_two(kept, got):
-        sums = []
+    def passed_on(kept, got):
+        return [(kept[j][quarter:] + got[j][quarter:].astype(F32)).astype(BF16) for j in range(local)]
+
+    def step_two(kept, got, passed):
+        last = [over_dp(passed[j], second[j]) for j in range(local)]
+        return [
+            kept[j][:quarter] + got[j][:quarter].astype(F32) + last[j].astype(F32) for j in range(local)
+        ]
+
+    def along_second(value):
+        return [over_dp(value[j], second[j]) for j in range(local)]
+
+    def along_first(value):
+        return [over_dp(value[j], first[j]) for j in range(local)]
+
+    def rows_of(pieces, weight, dim, added=None, waits=()):
+        return [
+            back_to_rows(pieces[j], weight, j, dim, added[j] if added else (), waits) for j in range(local)
+        ]
+
+    def outer_all(source, pieces, shape, x_first, waits=(), brief=False):
+        total = ()
         for j in range(local):
-            passed = (kept[j][quarter:] + got[j][quarter:].astype(F32)).astype(BF16)
-            last = over_dp(passed, second[j])
-            sums.append(kept[j][:quarter] + got[j][:quarter].astype(F32) + last.astype(F32))
-        return sums
-
-    def gather_rows(owned):
-        full = []
-        for j in range(local):
-            a = owned[j]
-            b = over_dp(a, second[j])
-            c = over_dp(a, first[j])
-            d = over_dp(b, first[j])
-            full.append((a, b, c, d))
-        return full
-
-    def joined(pieces):
-        return [jnp.concatenate(p, axis=0) for p in pieces]
-
-    def share_rows(value):
-        stacked = jnp.stack(value)
-        width = stacked.shape[-1]
+            total = (outer(source[j], pieces[j], shape, j, total, x_first, waits, brief),)
+        return total[0]
+
+    def share_blocks(value):
+        width = value[0][0].shape[-1]
         if paired:
-            summed = stacked[:, :half] + other_core(stacked[:, half:])
+            summed = jnp.stack([low + other_core(high) for low, high in value])
         else:
+            stacked = jnp.stack([jnp.concatenate(v, axis=0) for v in value])
             summed = lax.psum_scatter(stacked, "tensor", scatter_dimension=1, tiled=True)
         inner = min(share, part)
         summed = summed.astype(BF16).reshape(local, share // inner, groups, inner, width)
         blocks = summed.transpose(2, 0, 1, 3, 4).reshape(groups, local, share, width)
-        home = [blocks[0]] + [over_groups(blocks[k], -k) for k in range(1, groups)]
-        return jnp.stack(home).reshape(groups * local * share, width)
+        return [blocks[k] for k in range(groups)]
+
+    def return_home(blocks):
+        return [blocks[0]] + [over_groups(blocks[k], -k) for k in range(1, groups)]
 
     def to_tokens(home):
         if paired:
@@ -140,24 +283,30 @@
 
     inputs = take_in(send_out(tokens))
     gate_sent = send_half(inputs, w_gate, 0)
+    gate_sent = list(lax.optimization_barrier(tuple(gate_sent)))
     gate_got = step_one(gate_sent)
-    grads_out = send_out(after(grad_out, inputs))
     up_sent = send_half(inputs, w_up, 0)
+    up_sent = list(lax.optimization_barrier(tuple(up_sent)))
     up_got = step_one(up_sent)
-    gate_kept = keep_half(after(inputs, up_sent), w_gate, 0)
-    grad_rows = take_in(after(grads_out, gate_kept))
+    grads_out = send_out(held(grad_out, *gate_sent))
+    gate_kept = keep_half(inputs, w_gate, 0)
+    gate_passed = passed_on(gate_kept, gate_got)
+    gate_sum = step_two(gate_kept, gate_got, gate_passed)
+    grad_rows = take_in(grads_out)
     up_kept = keep_half(inputs, w_up, 0)
     back_sent = send_half(grad_rows, w_down, 1)
-    back_got = step_one(after(back_sent, gate_got))
-    gate_sum = step_two(gate_kept, gate_got)
+    back_sent = list(lax.optimization_barrier(tuple(back_sent)))
+    back_got = step_one(back_sent)
     back_kept = keep_half(grad_rows, w_down, 1)
-    up_sum = step_two(up_kept, up_got)
+    up_passed = passed_on(up_kept, up_got)
+    up_sum = step_two(up_kept, up_got, up_passed)
+    back_passed = passed_on(back_kept, back_got)
 
     hidden = []
     for j in range(local):
         hidden.append((gate_sum[j] * jax.nn.sigmoid(gate_sum[j]) * up_sum[j]).astype(BF16))
-    hidden_pieces = gather_rows(hidden)
-    back_sum = step_two(back_kept, back_got)
+    h_second, h_first = along_second(hidden), along_first(hidden)
+    back_sum = step_two(back_kept, back_got, back_passed)
     d_gate, d_up = [], []
     for j in range(local):
         g, u, b = gate_sum[j], up_sum[j], back_sum[j]
@@ -165,25 +314,30 @@
         d_gate.append((b * u * (s * (1.0 + g * (1.0 - s)))).astype(BF16))
         d_up.append((b * (g * s)).astype(BF16))
 
-    gate_pieces = gather_rows(after(d_gate, [p[2] for p in hidden_pieces]))
-    hidden_rows = joined(hidden_pieces)
-    forward = [dot(hidden_rows[j], w_down[j], 1, 0) for j in range(local)]
-    mixed = to_tokens(share_rows(forward))
-    up_pieces = gather_rows(after(d_up, [p[2] for p in gate_pieces]))
-    gate_rows = joined(gate_pieces)
-    up_rows = joined(up_pieces)
-    backward = [dot(gate_rows[j], w_gate[j], 1, 1) + dot(up_rows[j], w_up[j], 1, 1) for j in range(local)]
-
-    def outer(left, right):
-        return jnp.einsum(
-            "jrd,jrf->jdf", jnp.stack(left), jnp.stack(right), preferred_element_type=F32
-        ).astype(BF16)
-
-    grad_down = outer(hidden_rows, grad_rows)
-    grad_gate = outer(inputs, after(gate_rows, mixed))
-    grad_home = share_rows(backward)
-    grad_up = outer(inputs, after(up_rows, backward))
-    grad_tokens = to_tokens(grad_home)
+    h_both = along_first(h_second)
+    late = [held(v, *h_both) for v in d_gate]
+    g_second, g_first = along_second(late), along_first(late)
+    hidden_pieces = list(zip(hidden, h_second, h_first, h_both))
+    forward = rows_of(hidden_pieces, w_down, 0, None, g_second)
+    g_both = along_first(g_second)
+    late = d_up
+    u_second, u_first = along_second(late), along_first(late)
+    grad_down = outer_all(grad_rows, hidden_pieces, w_down.shape, False, [f[0] for f in forward] + u_second)
+    gate_pieces = list(zip(d_gate, g_second, g_first, g_both))
+    by_gate = rows_of(gate_pieces, w_gate, 1, None, ())
+    inputs_t = [x.T for x in inputs]
+    grad_gate = outer_all(inputs_t, gate_pieces, w_gate.shape, True, [grad_down])
+    u_both = along_first([held(v, *[grad_down]) for v in u_second])
+    mixed_home = jnp.stack(return_home(share_blocks([(held(low, *g_both), high) for low, high in forward]))).reshape(
+        groups * local * share, -1
+    )
+    mixed = to_tokens(mixed_home)
+    up_pieces = list(zip(d_up, u_second, u_first, u_both))
+    backward = rows_of(up_pieces, w_up, 1, by_gate, [grad_gate] + [mixed])
+    grad_blocks = share_blocks(backward)
+    grad_up = outer_all(inputs_t, up_pieces, w_up.shape, True, [spaced(*grad_blocks)], True)
+    grad_home = gathered(return_home(grad_blocks), [grad_up])
+    grad_tokens = to_tokens(grad_home.reshape(groups * local * share, -1))
     return mixed, grad_tokens, grad_gate, grad_up, grad_down
 
 

time: 422 us -> 414 us (0.981)
  Pallas kernels: 0 us -> 107 us
  matrix products: 140 us -> 59.2 us
  waiting for transfers between devices: 196 us -> 137 us
  starting transfers between devices: 52.8 us -> 67.4 us
  local copies, waits for them, and re-layouts: 9.83 us -> 17.6 us
    pallas_call x0 -> x21, Pallas kernels: none -> 107 us  [the longest x6 46.8 us: outer(): pl.pallas_call(kernel, grid=(width // tile,), in_specs=[pl.BlockSpec(x.sh...]
    ppermute x30, waiting for transfers between devices: 156 us -> 111 us  [over_dp(): return lax.ppermute(value, 'dp', [(i, i ^ bit) for i in range(peers)])]
    dot_general x23 -> x17, matrix products: 102 us -> 59.2 us  [dot(): lax.dot_general(lhs, rhs, (((lhs_dim,), (rhs_dim,)), ((), ())), preferred...]
    dot_general x3 -> x0, matrix products: 38 us -> none  [outer(): jnp.einsum('jrd,jrf->jdf', jnp.stack(left), jnp.stack(right), preferred_e...]
    ppermute x12, waiting for transfers between devices: 37.4 us -> 19.8 us  [over_groups(): lax.ppermute(value, 'expert', [(i, (i + shift) % groups) for i in range(g...]
    ppermute x30, starting transfers between devices: 20.8 us -> 30.2 us  [over_dp(): return lax.ppermute(value, 'dp', [(i, i ^ bit) for i in range(peers)])]
    unnamed x58 -> x94, local copies, waits for them, and re-layouts: 4.07 us -> 10.4 us
    convert_element_type x10 -> x8, other arithmetic: 7.64 us -> 13 us  [the longest x2 7.47 us: body(): d_up.append((b * (g * s)).astype(BF16))]
  transfers between devices with their start and end apart: 48 -> 50, of which waited for: 21 -> 18; matrix products, arithmetic and copies ran while one was open for 35% -> 14% of each run, Pallas kernels for 0% -> 26%
where the time goes in v2:
time: 414 us; the launch traced here: 406 us
  waiting for transfers between devices  137 us (33%)
  Pallas kernels  107 us (26%)
  starting transfers between devices  67.4 us (16%)
  matrix products  59.2 us (14%)
  local copies, waits for them, and re-layouts  17.6 us (4%)
  other arithmetic  16.2 us (4%)
    ppermute x30, waiting for transfers between devices, over_dp(): return lax.ppermute(value, 'dp', [(i, i ^ bit) for i in range(peers)])  111 us
    dot_general x17, matrix products, dot(): lax.dot_general(lhs, rhs, (((lhs_dim,), (rhs_dim,)), ((), ())), preferred...  59.2 us
    pallas_call x6, Pallas kernels, outer(): pl.pallas_call(kernel, grid=(width // tile,), in_specs=[pl.BlockSpec(x.sh...  46.8 us
    pallas_call x6, Pallas kernels, back_to_rows(): pl.pallas_call(kernel, grid=(width // tile,), in_specs=[pl.BlockSpec((n,...  42.9 us
    ppermute x30, starting transfers between devices, over_dp(): return lax.ppermute(value, 'dp', [(i, i ^ bit) for i in range(peers)])  30.2 us
    ppermute x8, starting transfers between devices, other_core(): return lax.ppermute(value, 'tensor', [(0, 1), (1, 0)])  21.2 us
    ppermute x12, waiting for transfers between devices, over_groups(): lax.ppermute(value, 'expert', [(i, (i + shift) % groups) for i in range(g...  19.8 us
    ppermute x12, starting transfers between devices, over_groups(): lax.ppermute(value, 'expert', [(i, (i + shift) % groups) for i in range(g...  16 us
  transfers between devices with their start and end apart: 50, of which 18 were waited for; matrix products, arithmetic and copies ran while one was open for 14% of the time, Pallas kernels for 26%

profile of v2, /device:TPU:11, one launch (start us, length us, event | category | flops | bytes accessed | tf_op | source)
XLA Modules:
  0.0 406.1 jit_solution(6490615415493690294)
XLA Ops:
  7.2 11.5 %collective-permute-done.1 = bf16[2,48,1024]{2,1,0:T(8,128)(2,1)S(1)} collective-permute-done((bf16[2,48,1024]{2,1,0:T(8,128)(2,1)S(1)}, bf16[2,48,1024]{2,1,0:T(8,128)(2,1)S(1)}, u32[]{:S(2)}, u32[]{:S(2)}) %collective-permute-start.1) | collective-permute-done | bytes 196640 | tf_op jit(solution)/shard_map/ppermute | solution.py:174
  27.0 6.6 %fusion.42 = bf16[192,3584]{1,0:T(8,128)(2,1)} fusion(bf16[192,1024]{1,0:T(8,128)(2,1)S(1)} %bitcast.178, bf16[2,1024,3584]{2,1,0:T(8,128)(2,1)} %refs_4_.11), kind=kOutput, calls=%fused_computation.38 | convolution fusion | flops 1409974272 | bytes 9109504 | tf_op jit(solution)/shard_map/dot_general | solution.py:14
  54.5 6.4 %fusion.8 = f32[192,3584]{1,0:T(8,128)} fusion(bf16[192,1024]{1,0:T(8,128)(2,1)S(1)} %bitcast.169, bf16[2,1024,3584]{2,1,0:T(8,128)(2,1)} %refs_4_.11), kind=kOutput, calls=%fused_computation.8 | convolution fusion | flops 1409286144 | bytes 10485760 | tf_op jit(solution)/shard_map/dot_general | solution.py:14
  96.0 10.3 %collective-permute-done.19 = bf16[192,3584]{1,0:T(8,128)(2,1)} collective-permute-done((bf16[192,3584]{1,0:T(8,128)(2,1)}, bf16[192,3584]{1,0:T(8,128)(2,1)}, u32[]{:S(2)}, u32[]{:S(2)}) %collective-permute-start.19) | collective-permute-done | bytes 1376288 | tf_op jit(solution)/shard_map/ppermute | solution.py:171
  115.0 21.4 %collective-permute-done.24 = bf16[192,3584]{1,0:T(8,128)(2,1)S(1)} collective-permute-done((bf16[192,3584]{1,0:T(8,128)(2,1)S(1)}, bf16[192,3584]{1,0:T(8,128)(2,1)S(1)}, u32[]{:S(2)}, u32[]{:S(2)}) %collective-permute-start.24) | collective-permute-done | bytes 1376288 | tf_op jit(solution)/shard_map/ppermute | solution.py:171
  139.4 11.1 %collective-permute-done.20 = bf16[96,3584]{1,0:T(8,128)(2,1)S(1)} collective-permute-done((bf16[96,3584]{1,0:T(8,128)(2,1)S(1)}, bf16[96,3584]{1,0:T(8,128)(2,1)S(1)}, u32[]{:S(2)}, u32[]{:S(2)}) %collective-permute-start.20) | collective-permute-done | bytes 688160 | tf_op jit(solution)/shard_map/ppermute | solution.py:171
  151.8 13.4 %collective-permute-done.18 = bf16[96,3584]{1,0:T(8,128)(2,1)S(1)} collective-permute-done((bf16[96,3584]{1,0:T(8,128)(2,1)S(1)}, bf16[96,3584]{1,0:T(8,128)(2,1)S(1)}, u32[]{:S(2)}, u32[]{:S(2)}) %collective-permute-start.18) | collective-permute-done | bytes 688160 | tf_op jit(solution)/shard_map/ppermute | solution.py:171
  165.3 14.7 %collective-permute-done.25 = bf16[96,3584]{1,0:T(8,128)(2,1)S(1)} collective-permute-done((bf16[96,3584]{1,0:T(8,128)(2,1)S(1)}, bf16[96,3584]{1,0:T(8,128)(2,1)S(1)}, u32[]{:S(2)}, u32[]{:S(2)}) %collective-permute-start.25) | collective-permute-done | bytes 688160 | tf_op jit(solution)/shard_map/ppermute | solution.py:171
  189.1 10.5 %collective-permute-done.21.refs_1_.refs_2_ = bf16[96,3584]{1,0:T(8,128)(2,1)S(1)} collective-permute-done((bf16[96,3584]{1,0:T(8,128)(2,1)}, bf16[96,3584]{1,0:T(8,128)(2,1)S(1)}, u32[]{:S(2)}, u32[]{:S(2)}) %collective-permute-start.21) | collective-permute-done | bytes 688160 | tf_op jit(solution)/shard_map/ppermute | solution.py:171
  206.0 12.1 %collective-permute-done.22.refs_2_.refs_3_.refs_4_ = bf16[96,3584]{1,0:T(8,128)(2,1)S(1)} collective-permute-done((bf16[96,3584]{1,0:T(8,128)(2,1)S(1)}, bf16[96,3584]{1,0:T(8,128)(2,1)S(1)}, u32[]{:S(2)}, u32[]{:S(2)}) %collective-permute-start.22) | collective-permute-done | bytes 688160 | tf_op jit(solution)/shard_map/ppermute | solution.py:171
  234.4 13.2 %collective-permute-done.23.refs_5_.refs_1_.refs_2_ = bf16[96,3584]{1,0:T(8,128)(2,1)} collective-permute-done((bf16[96,3584]{1,0:T(8,128)(2,1)}, bf16[96,3584]{1,0:T(8,128)(2,1)}, u32[]{:S(2)}, u32[]{:S(2)}) %collective-permute-start.23) | collective-permute-done | bytes 688160 | tf_op jit(solution)/shard_map/ppermute | solution.py:171
  247.7 6.9 %back_to_rows.7 = (f32[192,1024]{1,0:T(8,128)}, f32[192,1024]{1,0:T(8,128)}) custom-call(bf16[96,3584]{1,0:T(8,128)(2,1)} %get-tuple-element.46.refs_0_.refs_1_, bf16[96,3584]{1,0:T(8,128)(2,1)} %copy-done.22, bf16[96,3584]{1,0:T(8,128)(2,1)} %collective-permute-done.30.refs_2_.refs_3_, bf16[96,3584]{1,0:T(8,128)(2,1)} %copy-done.11, ...), custom_call_target="tpu_custom_call" | custom-call | flops 2818572288 | bytes 11665408 | tf_op jit(solution)/shard_map/back_to_rows/pallas_call | solution.py:63
  261.6 6.9 %back_to_rows.6 = (f32[192,1024]{1,0:T(8,128)}, f32[192,1024]{1,0:T(8,128)}) custom-call(bf16[96,3584]{1,0:T(8,128)(2,1)} %get-tuple-element.43.refs_0_.refs_1_, bf16[96,3584]{1,0:T(8,128)(2,1)} %copy-done.17, bf16[96,3584]{1,0:T(8,128)(2,1)} %collective-permute-done.9.refs_2_.refs_3_, bf16[96,3584]{1,0:T(8,128)(2,1)} %copy-done.9, ...), custom_call_target="tpu_custom_call" | custom-call | flops 2818572288 | bytes 11665408 | tf_op jit(solution)/shard_map/back_to_rows/pallas_call | solution.py:63
  268.4 8.9 %collective-permute-start.29 = (f32[192,1024]{1,0:T(8,128)}, f32[192,1024]{1,0:T(8,128)}, u32[]{:S(2)}, u32[]{:S(2)}) collective-permute-start(f32[192,1024]{1,0:T(8,128)} %get-tuple-element.30), channel_id=1, source_target_pairs={{0,1},{1,0},{2,3},{3,2},{4,5},{5,4},{6,7},{7,6},{8,9},{9,8},{10,11... | collective-permute-start | bytes 2359304 | tf_op jit(solution)/shard_map/ppermute | solution.py:177
  280.7 7.9 %outer.6.refs_5_ = bf16[2,3584,1024]{2,1,0:T(8,128)(2,1)} custom-call(bf16[384,1024]{1,0:T(8,128)(2,1)} %bitcast.130, bf16[96,3584]{1,0:T(8,128)(2,1)} %get-tuple-element.43.refs_0_.refs_1_, bf16[96,3584]{1,0:T(8,128)(2,1)} %copy-done.17, bf16[96,3584]{1,0:T(8,128)(2,1)} %collective-permute-done.9.refs_2_.refs_3_, bf16[96,3584]{1,0:T(8,128)(2,1)} %copy-done.9, ...), custom_call_target="tpu_custom_call" | custom-call | flops 2818572288 | bytes 10092544 | tf_op jit(solution)/shard_map/outer/pallas_call | solution.py:94
  300.9 7.8 %outer.7.refs_1_.refs_5_.refs_6_ = bf16[2,3584,1024]{2,1,0:T(8,128)(2,1)} custom-call(bf16[384,1024]{1,0:T(8,128)(2,1)} %bitcast.133, bf16[96,3584]{1,0:T(8,128)(2,1)} %get-tuple-element.46.refs_0_.refs_1_, bf16[96,3584]{1,0:T(8,128)(2,1)} %copy-done.22, bf16[96,3584]{1,0:T(8,128)(2,1)} %collective-permute-done.30.refs_2_.refs_3_, ...), custom_call_target="tpu_custom_call", output_to_operand_aliasing={{}: (5, {})} | custom-call | flops 2818572288 | bytes 10092544 | tf_op jit(solution)/shard_map/outer/pallas_call | solution.py:94
  319.2 6.9 %back_to_rows.8 = (f32[192,1024]{1,0:T(8,128)}, f32[192,1024]{1,0:T(8,128)}) custom-call(bf16[96,3584]{1,0:T(8,128)(2,1)} %get-tuple-element.42.refs_0_.refs_1_, bf16[96,3584]{1,0:T(8,128)(2,1)} %collective-permute-done.23.refs_5_.refs_1_.refs_2_, bf16[96,3584]{1,0:T(8,128)(2,1)} %copy-done.26, bf16[96,3584]{1,0:T(8,128)(2,1)} %copy-done.12, ...), custom_call_target="tpu_custom_call" | custom-call | flops 2818572288 | bytes 11665408 | tf_op jit(solution)/shard_map/back_to_rows/pallas_call | solution.py:63
  326.1 7.8 %outer.8.refs_5_ = bf16[2,1024,3584]{2,1,0:T(8,128)(2,1)} custom-call(bf16[1024,384]{1,0:T(8,128)(2,1)} %bitcast.126, bf16[96,3584]{1,0:T(8,128)(2,1)} %get-tuple-element.42.refs_0_.refs_1_, bf16[96,3584]{1,0:T(8,128)(2,1)} %collective-permute-done.23.refs_5_.refs_1_.refs_2_, bf16[96,3584]{1,0:T(8,128)(2,1)} %copy-done.26, bf16[96,3584]{1,0:T(8,128)(2,1)} %copy-done.12, ...), custom_call_target="tpu_custom_call" | custom-call | flops 2818572288 | bytes 10092544 | tf_op jit(solution)/shard_map/outer/pallas_call | solution.py:94
  334.8 7.8 %outer.9.refs_7_ = bf16[2,1024,3584]{2,1,0:T(8,128)(2,1)} custom-call(bf16[1024,384]{1,0:T(8,128)(2,1)} %bitcast.128, bf16[96,3584]{1,0:T(8,128)(2,1)} %get-tuple-element.45.refs_0_.refs_1_, bf16[96,3584]{1,0:T(8,128)(2,1)} %collective-permute-done.26.refs_6_.refs_2_.refs_1_, bf16[96,3584]{1,0:T(8,128)(2,1)} %copy-done.23, ...), custom_call_target="tpu_custom_call", output_to_operand_aliasing={{}: (5, {})} | custom-call | flops 2818572288 | bytes 10092544 | tf_op jit(solution)/shard_map/outer/pallas_call | solution.py:94
  345.7 7.6 %back_to_rows.9 = (f32[192,1024]{1,0:T(8,128)}, f32[192,1024]{1,0:T(8,128)}) custom-call(bf16[96,3584]{1,0:T(8,128)(2,1)} %get-tuple-element.41.refs_0_.refs_1_, bf16[96,3584]{1,0:T(8,128)(2,1)} %copy-done.3, bf16[96,3584]{1,0:T(8,128)(2,1)} %copy-done.24, bf16[96,3584]{1,0:T(8,128)(2,1)} %copy-done.25, bf16[2,1024,3584]{2,1,0:T(8,128)(2,1)} %refs_4_.11, ...), custom_call_target="tpu_custom_call" | custom-call | flops 2818572288 | bytes 11665408 | tf_op jit(solution)/shard_map/back_to_rows/pallas_call | solution.py:63
  356.0 6.9 %back_to_rows.10 = (f32[192,1024]{1,0:T(8,128)}, f32[192,1024]{1,0:T(8,128)}) custom-call(bf16[96,3584]{1,0:T(8,128)(2,1)} %get-tuple-element.45.refs_0_.refs_1_, bf16[96,3584]{1,0:T(8,128)(2,1)} %collective-permute-done.26.refs_6_.refs_2_.refs_1_, bf16[96,3584]{1,0:T(8,128)(2,1)} %copy-done.23, bf16[96,3584]{1,0:T(8,128)(2,1)} %copy-done.10, ...), custom_call_target="tpu_custom_call" | custom-call | flops 2818572288 | bytes 11665408 | tf_op jit(solution)/shard_map/back_to_rows/pallas_call | solution.py:63
  364.0 7.7 %back_to_rows.11 = (f32[192,1024]{1,0:T(8,128)}, f32[192,1024]{1,0:T(8,128)}) custom-call(bf16[96,3584]{1,0:T(8,128)(2,1)} %get-tuple-element.44.refs_0_.refs_1_, bf16[96,3584]{1,0:T(8,128)(2,1)} %copy-done.4, bf16[96,3584]{1,0:T(8,128)(2,1)} %copy-done.27, bf16[96,3584]{1,0:T(8,128)(2,1)} %copy-done.28, bf16[2,1024,3584]{2,1,0:T(8,128)(2,1)} %refs_4_.11, ...), custom_call_target="tpu_custom_call" | custom-call | flops 2818572288 | bytes 11665408 | tf_op jit(solution)/shard_map/back_to_rows/pallas_call | solution.py:63
  380.4 7.8 %outer.10.refs_5_ = bf16[2,1024,3584]{2,1,0:T(8,128)(2,1)} custom-call(bf16[1024,384]{1,0:T(8,128)(2,1)} %bitcast.127, bf16[96,3584]{1,0:T(8,128)(2,1)} %get-tuple-element.41.refs_0_.refs_1_, bf16[96,3584]{1,0:T(8,128)(2,1)} %copy-done.3, bf16[96,3584]{1,0:T(8,128)(2,1)} %copy-done.24, bf16[96,3584]{1,0:T(8,128)(2,1)} %copy-done.25, ...), custom_call_target="tpu_custom_call" | custom-call | tf_op jit(solution)/shard_map/outer/pallas_call | solution.py:94
  388.2 7.8 %outer.11.refs_4_ = bf16[2,1024,3584]{2,1,0:T(8,128)(2,1)} custom-call(bf16[1024,384]{1,0:T(8,128)(2,1)} %bitcast.129, bf16[96,3584]{1,0:T(8,128)(2,1)} %get-tuple-element.44.refs_0_.refs_1_, bf16[96,3584]{1,0:T(8,128)(2,1)} %copy-done.4, bf16[96,3584]{1,0:T(8,128)(2,1)} %copy-done.27, bf16[96,3584]{1,0:T(8,128)(2,1)} %copy-done.28, ...), custom_call_target="tpu_custom_call", output_to_operand_aliasing={{}: (5, {})} | custom-call | tf_op jit(solution)/shard_map/outer/pallas_call | solution.py:94
  (263 shorter events, 174.8 us)
Async XLA Ops:
  45.2 68.4 %collective-permute-start.4 = (bf16[192,3584]{1,0:T(8,128)(2,1)}, bf16[192,3584]{1,0:T(8,128)(2,1)}, u32[]{:S(2)}, u32[]{:S(2)}) collective-permute-start(bf16[192,3584]{1,0:T(8,128)(2,1)} %fusion.36.refs_1_), channel_id=1, source_target_pairs={{0,8},{8,0},{16,24},{24,16},{1,9},{9,1},{17,25},{25,17},{2,10},{10... | collective-permute-start | bytes 4128776 | tf_op jit(solution)/shard_map/ppermute | solution.py:171
  45.5 63.5 %collective-permute-start.17 = (bf16[192,3584]{1,0:T(8,128)(2,1)}, bf16[192,3584]{1,0:T(8,128)(2,1)}, u32[]{:S(2)}, u32[]{:S(2)}) collective-permute-start(bf16[192,3584]{1,0:T(8,128)(2,1)} %fusion.39.refs_2_), channel_id=1, source_target_pairs={{0,16},{8,24},{16,0},{24,8},{1,17},{9,25},{17,1},{25,9},{2,18},{10... | collective-permute-start | bytes 4128776 | tf_op jit(solution)/shard_map/ppermute | solution.py:171
  67.3 44.2 %collective-permute-start.6 = (bf16[192,3584]{1,0:T(8,128)(2,1)}, bf16[192,3584]{1,0:T(8,128)(2,1)}, u32[]{:S(2)}, u32[]{:S(2)}) collective-permute-start(bf16[192,3584]{1,0:T(8,128)(2,1)} %fusion.42), channel_id=1, source_target_pairs={{0,8},{8,0},{16,24},{24,16},{1,9},{9,1},{17,25},{25,17},{2,10},{10... | collective-permute-start | bytes 4128776 | tf_op jit(solution)/shard_map/ppermute | solution.py:171
  71.1 35.2 %collective-permute-start.19 = (bf16[192,3584]{1,0:T(8,128)(2,1)}, bf16[192,3584]{1,0:T(8,128)(2,1)}, u32[]{:S(2)}, u32[]{:S(2)}) collective-permute-start(bf16[192,3584]{1,0:T(8,128)(2,1)} %fusion.45), channel_id=1, source_target_pairs={{0,16},{8,24},{16,0},{24,8},{1,17},{9,25},{17,1},{25,9},{2,18},{10... | collective-permute-start | bytes 4128776 | tf_op jit(solution)/shard_map/ppermute | solution.py:171
  89.6 48.4 %collective-permute-start.15 = (bf16[192,3584]{1,0:T(8,128)(2,1)S(1)}, bf16[192,3584]{1,0:T(8,128)(2,1)S(1)}, u32[]{:S(2)}, u32[]{:S(2)}) collective-permute-start(bf16[192,3584]{1,0:T(8,128)(2,1)S(1)} %fusion.48), channel_id=1, source_target_pairs={{0,8},{8,0},{16,24},{24,16},{1,9},{9,1},{17,25},{25,17},{2,10},{10... | collective-permute-start | bytes 4128776 | tf_op jit(solution)/shard_map/ppermute | solution.py:171
  106.3 30.1 %collective-permute-start.24 = (bf16[192,3584]{1,0:T(8,128)(2,1)S(1)}, bf16[192,3584]{1,0:T(8,128)(2,1)S(1)}, u32[]{:S(2)}, u32[]{:S(2)}) collective-permute-start(bf16[192,3584]{1,0:T(8,128)(2,1)S(1)} %fusion.51), channel_id=1, source_target_pairs={{0,16},{8,24},{16,0},{24,8},{1,17},{9,25},{17,1},{25,9},{2,18},{10... | collective-permute-start | bytes 4128776 | tf_op jit(solution)/shard_map/ppermute | solution.py:171
  109.0 41.5 %collective-permute-start.20 = (bf16[96,3584]{1,0:T(8,128)(2,1)S(1)}, bf16[96,3584]{1,0:T(8,128)(2,1)S(1)}, u32[]{:S(2)}, u32[]{:S(2)}) collective-permute-start(bf16[96,3584]{1,0:T(8,128)(2,1)S(1)} %fusion.76), channel_id=1, source_target_pairs={{0,8},{8,0},{16,24},{24,16},{1,9},{9,1},{17,25},{25,17},{2,10},{10... | collective-permute-start | bytes 2064392 | tf_op jit(solution)/shard_map/ppermute | solution.py:171
  111.5 53.8 %collective-permute-start.18 = (bf16[96,3584]{1,0:T(8,128)(2,1)S(1)}, bf16[96,3584]{1,0:T(8,128)(2,1)S(1)}, u32[]{:S(2)}, u32[]{:S(2)}) collective-permute-start(bf16[96,3584]{1,0:T(8,128)(2,1)S(1)} %fusion.78), channel_id=1, source_target_pairs={{0,8},{8,0},{16,24},{24,16},{1,9},{9,1},{17,25},{25,17},{2,10},{10... | collective-permute-start | bytes 2064392 | tf_op jit(solution)/shard_map/ppermute | solution.py:171
  113.6 70.4 %collective-permute-start.7 = (bf16[96,3584]{1,0:T(8,128)(2,1)S(1)}, bf16[96,3584]{1,0:T(8,128)(2,1)S(1)}, u32[]{:S(2)}, u32[]{:S(2)}) collective-permute-start(bf16[96,3584]{1,0:T(8,128)(2,1)S(1)} %fusion.82), channel_id=1, source_target_pairs={{0,16},{8,24},{16,0},{24,8},{1,17},{9,25},{17,1},{25,9},{2,18},{10... | collective-permute-start | bytes 2064392 | tf_op jit(solution)/shard_map/ppermute | solution.py:171
  136.4 47.6 %collective-permute-start.5 = (bf16[96,3584]{1,0:T(8,128)(2,1)S(1)}, bf16[96,3584]{1,0:T(8,128)(2,1)S(1)}, u32[]{:S(2)}, u32[]{:S(2)}) collective-permute-start(bf16[96,3584]{1,0:T(8,128)(2,1)S(1)} %fusion.84), channel_id=1, source_target_pairs={{0,16},{8,24},{16,0},{24,8},{1,17},{9,25},{17,1},{25,9},{2,18},{10... | collective-permute-start | bytes 2064392 | tf_op jit(solution)/shard_map/ppermute | solution.py:171
  138.1 41.9 %collective-permute-start.25 = (bf16[96,3584]{1,0:T(8,128)(2,1)S(1)}, bf16[96,3584]{1,0:T(8,128)(2,1)S(1)}, u32[]{:S(2)}, u32[]{:S(2)}) collective-permute-start(bf16[96,3584]{1,0:T(8,128)(2,1)S(1)} %fusion.74), channel_id=1, source_target_pairs={{0,8},{8,0},{16,24},{24,16},{1,9},{9,1},{17,25},{25,17},{2,10},{10... | collective-permute-start | bytes 2064392 | tf_op jit(solution)/shard_map/ppermute | solution.py:171
  150.5 33.4 %collective-permute-start.16 = (bf16[96,3584]{1,0:T(8,128)(2,1)S(1)}, bf16[96,3584]{1,0:T(8,128)(2,1)S(1)}, u32[]{:S(2)}, u32[]{:S(2)}) collective-permute-start(bf16[96,3584]{1,0:T(8,128)(2,1)S(1)} %fusion.80), channel_id=1, source_target_pairs={{0,16},{8,24},{16,0},{24,8},{1,17},{9,25},{17,1},{25,9},{2,18},{10... | collective-permute-start | bytes 2064392 | tf_op jit(solution)/shard_map/ppermute | solution.py:171
  225.8 34.5 %collective-permute-start.9 = (bf16[96,3584]{1,0:T(8,128)(2,1)}, bf16[96,3584]{1,0:T(8,128)(2,1)}, u32[]{:S(2)}, u32[]{:S(2)}) collective-permute-start(bf16[96,3584]{1,0:T(8,128)(2,1)} %get-tuple-element.43.refs_0_.refs_1_), channel_id=1, source_target_pairs={{0,8},{8,0},{16,24},{24,16},{1,9},{9,1},{17,25},{25,17},{2,10},{10... | collective-permute-start | bytes 2064392 | tf_op jit(solution)/shard_map/ppermute | solution.py:171
  226.3 42.2 %collective-permute-start.38 = (bf16[96,3584]{1,0:T(8,128)(2,1)}, bf16[96,3584]{1,0:T(8,128)(2,1)S(1)}, u32[]{:S(2)}, u32[]{:S(2)}) collective-permute-start(bf16[96,3584]{1,0:T(8,128)(2,1)} %get-tuple-element.44.refs_0_.refs_1_), channel_id=1, source_target_pairs={{0,8},{8,0},{16,24},{24,16},{1,9},{9,1},{17,25},{25,17},{2,10},{10... | collective-permute-start | bytes 2064392 | tf_op jit(solution)/shard_map/ppermute | solution.py:171
  232.9 46.5 %collective-permute-start.36 = (bf16[96,3584]{1,0:T(8,128)(2,1)S(1)}, bf16[96,3584]{1,0:T(8,128)(2,1)S(1)}, u32[]{:S(2)}, u32[]{:S(2)}) collective-permute-start(bf16[96,3584]{1,0:T(8,128)(2,1)S(1)} %copy-done.13), channel_id=1, source_target_pairs={{0,16},{8,24},{16,0},{24,8},{1,17},{9,25},{17,1},{25,9},{2,18},{10... | collective-permute-start | bytes 2064392 | tf_op jit(solution)/shard_map/ppermute | solution.py:171
  254.5 39.9 %collective-permute-start.31 = (f32[192,1024]{1,0:T(8,128)}, f32[192,1024]{1,0:T(8,128)S(1)}, u32[]{:S(2)}, u32[]{:S(2)}) collective-permute-start(f32[192,1024]{1,0:T(8,128)} %get-tuple-element.32), channel_id=1, source_target_pairs={{0,1},{1,0},{2,3},{3,2},{4,5},{5,4},{6,7},{7,6},{8,9},{9,8},{10,11... | collective-permute-start | bytes 2359304 | tf_op jit(solution)/shard_map/ppermute | solution.py:177
  259.1 29.4 %collective-permute-start.27 = (bf16[96,3584]{1,0:T(8,128)(2,1)}, bf16[96,3584]{1,0:T(8,128)(2,1)S(1)}, u32[]{:S(2)}, u32[]{:S(2)}) collective-permute-start(bf16[96,3584]{1,0:T(8,128)(2,1)} %collective-permute-done.23.refs_5_.refs_1_.refs_2_), channel_id=1, source_target_pairs={{0,8},{8,0},{16,24},{24,16},{1,9},{9,1},{17,25},{25,17},{2,10},{10... | collective-permute-start | bytes 2064392 | tf_op jit(solution)/shard_map/ppermute | solution.py:171
  260.3 28.5 %collective-permute-start.28 = (bf16[96,3584]{1,0:T(8,128)(2,1)}, bf16[96,3584]{1,0:T(8,128)(2,1)S(1)}, u32[]{:S(2)}, u32[]{:S(2)}) collective-permute-start(bf16[96,3584]{1,0:T(8,128)(2,1)} %collective-permute-done.26.refs_6_.refs_2_.refs_1_), channel_id=1, source_target_pairs={{0,16},{8,24},{16,0},{24,8},{1,17},{9,25},{17,1},{25,9},{2,18},{10... | collective-permute-start | bytes 2064392 | tf_op jit(solution)/shard_map/ppermute | solution.py:171
  279.5 37.0 %collective-permute-start.40 = (bf16[96,3584]{1,0:T(8,128)(2,1)}, bf16[96,3584]{1,0:T(8,128)(2,1)S(1)}, u32[]{:S(2)}, u32[]{:S(2)}) collective-permute-start(bf16[96,3584]{1,0:T(8,128)(2,1)} %held.8), channel_id=1, source_target_pairs={{0,8},{8,0},{16,24},{24,16},{1,9},{9,1},{17,25},{25,17},{2,10},{10... | collective-permute-start | bytes 2064392 | tf_op jit(solution)/shard_map/ppermute | solution.py:171
  288.5 45.4 %collective-permute-start.41 = (bf16[96,3584]{1,0:T(8,128)(2,1)}, bf16[96,3584]{1,0:T(8,128)(2,1)S(1)}, u32[]{:S(2)}, u32[]{:S(2)}) collective-permute-start(bf16[96,3584]{1,0:T(8,128)(2,1)} %held.9), channel_id=1, source_target_pairs={{0,16},{8,24},{16,0},{24,8},{1,17},{9,25},{17,1},{25,9},{2,18},{10... | collective-permute-start | bytes 2064392 | tf_op jit(solution)/shard_map/ppermute | solution.py:171
  312.7 50.2 %collective-permute-start.43 = (bf16[96,3584]{1,0:T(8,128)(2,1)}, bf16[96,3584]{1,0:T(8,128)(2,1)S(1)}, u32[]{:S(2)}, u32[]{:S(2)}) collective-permute-start(bf16[96,3584]{1,0:T(8,128)(2,1)} %get-tuple-element.44.refs_0_.refs_1_), channel_id=1, source_target_pairs={{0,16},{8,24},{16,0},{24,8},{1,17},{9,25},{17,1},{25,9},{2,18},{10... | collective-permute-start | bytes 2064392 | tf_op jit(solution)/shard_map/ppermute | solution.py:171
  314.9 29.7 %collective-permute-start.37 = (bf16[96,3584]{1,0:T(8,128)(2,1)S(1)}, bf16[96,3584]{1,0:T(8,128)(2,1)S(1)}, u32[]{:S(2)}, u32[]{:S(2)}) collective-permute-start(bf16[96,3584]{1,0:T(8,128)(2,1)S(1)} %copy-done.13), channel_id=1, source_target_pairs={{0,8},{8,0},{16,24},{24,16},{1,9},{9,1},{17,25},{25,17},{2,10},{10... | collective-permute-start | bytes 2064392 | tf_op jit(solution)/shard_map/ppermute | solution.py:171
  315.8 28.8 %collective-permute-start.39 = (bf16[96,3584]{1,0:T(8,128)(2,1)}, bf16[96,3584]{1,0:T(8,128)(2,1)S(1)}, u32[]{:S(2)}, u32[]{:S(2)}) collective-permute-start(bf16[96,3584]{1,0:T(8,128)(2,1)} %held.12), channel_id=1, source_target_pairs={{0,8},{8,0},{16,24},{24,16},{1,9},{9,1},{17,25},{25,17},{2,10},{10... | collective-permute-start | bytes 2064392 | tf_op jit(solution)/shard_map/ppermute | solution.py:171
  334.0 28.9 %collective-permute-start.44 = (bf16[96,3584]{1,0:T(8,128)(2,1)S(1)}, bf16[96,3584]{1,0:T(8,128)(2,1)S(1)}, u32[]{:S(2)}, u32[]{:S(2)}) collective-permute-start(bf16[96,3584]{1,0:T(8,128)(2,1)S(1)} %copy-done.34), channel_id=1, source_target_pairs={{0,16},{8,24},{16,0},{24,8},{1,17},{9,25},{17,1},{25,9},{2,18},{10... | collective-permute-start | bytes 2064392 | tf_op jit(solution)/shard_map/ppermute | solution.py:171
  (73 other events, 761.1 us)

commit v3 on v2

--- a/solution.py
+++ b/solution.py
@@ -327,7 +327,7 @@
     by_gate = rows_of(gate_pieces, w_gate, 1, None, ())
     inputs_t = [x.T for x in inputs]
     grad_gate = outer_all(inputs_t, gate_pieces, w_gate.shape, True, [grad_down])
-    u_both = along_first([held(v, *[grad_down]) for v in u_second])
+    u_both = along_first(u_second)
     mixed_home = jnp.stack(return_home(share_blocks([(held(low, *g_both), high) for low, high in forward]))).reshape(
         groups * local * share, -1
     )

time: 414 us -> 413 us (level)
  local copies, waits for them, and re-layouts: 17.6 us -> 22.4 us
    pallas_call x7 -> x5, Pallas kernels: 14.5 us -> 10.5 us  [held(): pl.pallas_call(kernel, in_specs=[pl.BlockSpec(memory_space=pltpu.VMEM)] +...]
    unnamed x94 -> x96, local copies, waits for them, and re-layouts: 10.4 us -> 12 us
  transfers between devices with their start and end apart: 50 -> 50, of which waited for: 18 -> 18; matrix products, arithmetic and copies ran while one was open for 14% -> 15% of each run, Pallas kernels for 26% -> 25%
where the time goes in v3:
time: 413 us; the launch traced here: 405 us
  waiting for transfers between devices  139 us (34%)
  Pallas kernels  103 us (25%)
  starting transfers between devices  65.2 us (16%)
  matrix products  59.2 us (14%)
  local copies, waits for them, and re-layouts  22.4 us (5%)
  other arithmetic  15.1 us (4%)
    ppermute x30, waiting for transfers between devices, over_dp(): return lax.ppermute(value, 'dp', [(i, i ^ bit) for i in range(peers)])  109 us
    dot_general x17, matrix products, dot(): lax.dot_general(lhs, rhs, (((lhs_dim,), (rhs_dim,)), ((), ())), preferred...  59.2 us
    pallas_call x6, Pallas kernels, outer(): pl.pallas_call(kernel, grid=(width // tile,), in_specs=[pl.BlockSpec(x.sh...  46.9 us
    pallas_call x6, Pallas kernels, back_to_rows(): pl.pallas_call(kernel, grid=(width // tile,), in_specs=[pl.BlockSpec((n,...  42.9 us
    ppermute x30, starting transfers between devices, over_dp(): return lax.ppermute(value, 'dp', [(i, i ^ bit) for i in range(peers)])  29.6 us
    ppermute x12, waiting for transfers between devices, over_groups(): lax.ppermute(value, 'expert', [(i, (i + shift) % groups) for i in range(g...  23.7 us
    ppermute x8, starting transfers between devices, other_core(): return lax.ppermute(value, 'tensor', [(0, 1), (1, 0)])  19.6 us
    ppermute x12, starting transfers between devices, over_groups(): lax.ppermute(value, 'expert', [(i, (i + shift) % groups) for i in range(g...  15.9 us
  transfers between devices with their start and end apart: 50, of which 18 were waited for; matrix products, arithmetic and copies ran while one was open for 15% of the time, Pallas kernels for 25%

profile of v3, /device:TPU:11, one launch (start us, length us, event | category | flops | bytes accessed | tf_op | source)
XLA Modules:
  0.0 405.1 jit_solution(1733694951152769423)
XLA Ops:
  7.2 11.5 %collective-permute-done.1 = bf16[2,48,1024]{2,1,0:T(8,128)(2,1)S(1)} collective-permute-done((bf16[2,48,1024]{2,1,0:T(8,128)(2,1)S(1)}, bf16[2,48,1024]{2,1,0:T(8,128)(2,1)S(1)}, u32[]{:S(2)}, u32[]{:S(2)}) %collective-permute-start.1) | collective-permute-done | bytes 196640 | tf_op jit(solution)/shard_map/ppermute | solution.py:174
  27.0 6.6 %fusion.42 = bf16[192,3584]{1,0:T(8,128)(2,1)} fusion(bf16[192,1024]{1,0:T(8,128)(2,1)S(1)} %bitcast.178, bf16[2,1024,3584]{2,1,0:T(8,128)(2,1)} %refs_4_.11), kind=kOutput, calls=%fused_computation.38 | convolution fusion | flops 1409974272 | bytes 9109504 | tf_op jit(solution)/shard_map/dot_general | solution.py:14
  72.8 6.4 %fusion.14 = f32[192,3584]{1,0:T(8,128)} fusion(bf16[192,1024]{1,0:T(8,128)(2,1)S(1)} %bitcast.171, bf16[2,1024,3584]{2,1,0:T(8,128)(2,1)} %refs_4_.11), kind=kOutput, calls=%fused_computation.14 | convolution fusion | flops 1409286144 | bytes 10485760 | tf_op jit(solution)/shard_map/dot_general | solution.py:14
  96.0 10.3 %collective-permute-done.19 = bf16[192,3584]{1,0:T(8,128)(2,1)} collective-permute-done((bf16[192,3584]{1,0:T(8,128)(2,1)}, bf16[192,3584]{1,0:T(8,128)(2,1)}, u32[]{:S(2)}, u32[]{:S(2)}) %collective-permute-start.19) | collective-permute-done | bytes 1376288 | tf_op jit(solution)/shard_map/ppermute | solution.py:171
  115.0 21.4 %collective-permute-done.24 = bf16[192,3584]{1,0:T(8,128)(2,1)S(1)} collective-permute-done((bf16[192,3584]{1,0:T(8,128)(2,1)S(1)}, bf16[192,3584]{1,0:T(8,128)(2,1)S(1)}, u32[]{:S(2)}, u32[]{:S(2)}) %collective-permute-start.24) | collective-permute-done | bytes 1376288 | tf_op jit(solution)/shard_map/ppermute | solution.py:171
  139.5 11.0 %collective-permute-done.20 = bf16[96,3584]{1,0:T(8,128)(2,1)S(1)} collective-permute-done((bf16[96,3584]{1,0:T(8,128)(2,1)S(1)}, bf16[96,3584]{1,0:T(8,128)(2,1)S(1)}, u32[]{:S(2)}, u32[]{:S(2)}) %collective-permute-start.20) | collective-permute-done | bytes 688160 | tf_op jit(solution)/shard_map/ppermute | solution.py:171
  151.9 13.3 %collective-permute-done.18 = bf16[96,3584]{1,0:T(8,128)(2,1)S(1)} collective-permute-done((bf16[96,3584]{1,0:T(8,128)(2,1)S(1)}, bf16[96,3584]{1,0:T(8,128)(2,1)S(1)}, u32[]{:S(2)}, u32[]{:S(2)}) %collective-permute-start.18) | collective-permute-done | bytes 688160 | tf_op jit(solution)/shard_map/ppermute | solution.py:171
  165.2 14.7 %collective-permute-done.25 = bf16[96,3584]{1,0:T(8,128)(2,1)S(1)} collective-permute-done((bf16[96,3584]{1,0:T(8,128)(2,1)S(1)}, bf16[96,3584]{1,0:T(8,128)(2,1)S(1)}, u32[]{:S(2)}, u32[]{:S(2)}) %collective-permute-start.25) | collective-permute-done | bytes 688160 | tf_op jit(solution)/shard_map/ppermute | solution.py:171
  189.1 10.5 %collective-permute-done.21.refs_1_.refs_2_ = bf16[96,3584]{1,0:T(8,128)(2,1)S(1)} collective-permute-done((bf16[96,3584]{1,0:T(8,128)(2,1)}, bf16[96,3584]{1,0:T(8,128)(2,1)S(1)}, u32[]{:S(2)}, u32[]{:S(2)}) %collective-permute-start.21) | collective-permute-done | bytes 688160 | tf_op jit(solution)/shard_map/ppermute | solution.py:171
  206.1 12.0 %collective-permute-done.22.refs_2_.refs_3_.refs_4_ = bf16[96,3584]{1,0:T(8,128)(2,1)S(1)} collective-permute-done((bf16[96,3584]{1,0:T(8,128)(2,1)S(1)}, bf16[96,3584]{1,0:T(8,128)(2,1)S(1)}, u32[]{:S(2)}, u32[]{:S(2)}) %collective-permute-start.22) | collective-permute-done | bytes 688160 | tf_op jit(solution)/shard_map/ppermute | solution.py:171
  234.5 13.2 %collective-permute-done.23.refs_5_.refs_1_.refs_2_ = bf16[96,3584]{1,0:T(8,128)(2,1)S(1)} collective-permute-done((bf16[96,3584]{1,0:T(8,128)(2,1)}, bf16[96,3584]{1,0:T(8,128)(2,1)S(1)}, u32[]{:S(2)}, u32[]{:S(2)}) %collective-permute-start.23) | collective-permute-done | bytes 688160 | tf_op jit(solution)/shard_map/ppermute | solution.py:171
  249.4 6.9 %back_to_rows.7 = (f32[192,1024]{1,0:T(8,128)}, f32[192,1024]{1,0:T(8,128)}) custom-call(bf16[96,3584]{1,0:T(8,128)(2,1)} %get-tuple-element.46.refs_0_.refs_1_, bf16[96,3584]{1,0:T(8,128)(2,1)} %copy-done.24, bf16[96,3584]{1,0:T(8,128)(2,1)} %collective-permute-done.30.refs_2_.refs_3_, bf16[96,3584]{1,0:T(8,128)(2,1)} %copy-done.10, ...), custom_call_target="tpu_custom_call" | custom-call | flops 2818572288 | bytes 11665408 | tf_op jit(solution)/shard_map/back_to_rows/pallas_call | solution.py:63
  263.2 6.9 %back_to_rows.6 = (f32[192,1024]{1,0:T(8,128)}, f32[192,1024]{1,0:T(8,128)}) custom-call(bf16[96,3584]{1,0:T(8,128)(2,1)} %get-tuple-element.43.refs_0_.refs_1_, bf16[96,3584]{1,0:T(8,128)(2,1)} %copy-done.19, bf16[96,3584]{1,0:T(8,128)(2,1)} %collective-permute-done.9.refs_2_.refs_3_, bf16[96,3584]{1,0:T(8,128)(2,1)} %copy-done.7, ...), custom_call_target="tpu_custom_call" | custom-call | flops 2818572288 | bytes 11665408 | tf_op jit(solution)/shard_map/back_to_rows/pallas_call | solution.py:63
  270.0 7.4 %collective-permute-start.29 = (f32[192,1024]{1,0:T(8,128)}, f32[192,1024]{1,0:T(8,128)S(1)}, u32[]{:S(2)}, u32[]{:S(2)}) collective-permute-start(f32[192,1024]{1,0:T(8,128)} %get-tuple-element.30), channel_id=1, source_target_pairs={{0,1},{1,0},{2,3},{3,2},{4,5},{5,4},{6,7},{7,6},{8,9},{9,8},{10,11... | collective-permute-start | bytes 2359304 | tf_op jit(solution)/shard_map/ppermute | solution.py:177
  280.8 7.8 %outer.6.refs_5_ = bf16[2,3584,1024]{2,1,0:T(8,128)(2,1)} custom-call(bf16[384,1024]{1,0:T(8,128)(2,1)} %bitcast.130, bf16[96,3584]{1,0:T(8,128)(2,1)} %get-tuple-element.43.refs_0_.refs_1_, bf16[96,3584]{1,0:T(8,128)(2,1)} %copy-done.19, bf16[96,3584]{1,0:T(8,128)(2,1)} %collective-permute-done.9.refs_2_.refs_3_, bf16[96,3584]{1,0:T(8,128)(2,1)} %copy-done.7, ...), custom_call_target="tpu_custom_call" | custom-call | flops 2818572288 | bytes 10092544 | tf_op jit(solution)/shard_map/outer/pallas_call | solution.py:94
  299.8 7.9 %outer.7.refs_5_.refs_6_ = bf16[2,3584,1024]{2,1,0:T(8,128)(2,1)} custom-call(bf16[384,1024]{1,0:T(8,128)(2,1)} %bitcast.133, bf16[96,3584]{1,0:T(8,128)(2,1)} %get-tuple-element.46.refs_0_.refs_1_, bf16[96,3584]{1,0:T(8,128)(2,1)} %copy-done.24, bf16[96,3584]{1,0:T(8,128)(2,1)} %collective-permute-done.30.refs_2_.refs_3_, ...), custom_call_target="tpu_custom_call", output_to_operand_aliasing={{}: (5, {})} | custom-call | flops 2818572288 | bytes 10092544 | tf_op jit(solution)/shard_map/outer/pallas_call | solution.py:94
  318.2 6.9 %back_to_rows.8 = (f32[192,1024]{1,0:T(8,128)}, f32[192,1024]{1,0:T(8,128)}) custom-call(bf16[96,3584]{1,0:T(8,128)(2,1)} %get-tuple-element.42.refs_0_.refs_1_, bf16[96,3584]{1,0:T(8,128)(2,1)} %copy-done.9, bf16[96,3584]{1,0:T(8,128)(2,1)} %copy-done.28, bf16[96,3584]{1,0:T(8,128)(2,1)} %copy-done.12, bf16[2,1024,3584]{2,1,0:T(8,128)(2,1)} %refs_4_.10), custom_call_target="tpu_custom_call" | custom-call | flops 2818572288 | bytes 11665408 | tf_op jit(solution)/shard_map/back_to_rows/pallas_call | solution.py:63
  325.1 7.8 %outer.8.refs_5_ = bf16[2,1024,3584]{2,1,0:T(8,128)(2,1)} custom-call(bf16[1024,384]{1,0:T(8,128)(2,1)} %bitcast.126, bf16[96,3584]{1,0:T(8,128)(2,1)} %get-tuple-element.42.refs_0_.refs_1_, bf16[96,3584]{1,0:T(8,128)(2,1)} %copy-done.9, bf16[96,3584]{1,0:T(8,128)(2,1)} %copy-done.28, bf16[96,3584]{1,0:T(8,128)(2,1)} %copy-done.12, ...), custom_call_target="tpu_custom_call" | custom-call | flops 2818572288 | bytes 10092544 | tf_op jit(solution)/shard_map/outer/pallas_call | solution.py:94
  333.7 7.8 %outer.9.refs_7_ = bf16[2,1024,3584]{2,1,0:T(8,128)(2,1)} custom-call(bf16[1024,384]{1,0:T(8,128)(2,1)} %bitcast.128, bf16[96,3584]{1,0:T(8,128)(2,1)} %get-tuple-element.45.refs_0_.refs_1_, bf16[96,3584]{1,0:T(8,128)(2,1)} %copy-done.8, bf16[96,3584]{1,0:T(8,128)(2,1)} %copy-done.25, bf16[96,3584]{1,0:T(8,128)(2,1)} %copy-done.11, ...), custom_call_target="tpu_custom_call", output_to_operand_aliasing={{}: (5, {})} | custom-call | flops 2818572288 | bytes 10092544 | tf_op jit(solution)/shard_map/outer/pallas_call | solution.py:94
  344.6 7.6 %back_to_rows.9 = (f32[192,1024]{1,0:T(8,128)}, f32[192,1024]{1,0:T(8,128)}) custom-call(bf16[96,3584]{1,0:T(8,128)(2,1)} %get-tuple-element.41.refs_0_.refs_1_, bf16[96,3584]{1,0:T(8,128)(2,1)} %copy-done.13, bf16[96,3584]{1,0:T(8,128)(2,1)} %copy-done.26, bf16[96,3584]{1,0:T(8,128)(2,1)} %copy-done.27, bf16[2,1024,3584]{2,1,0:T(8,128)(2,1)} %refs_4_.11, ...), custom_call_target="tpu_custom_call" | custom-call | flops 2818572288 | bytes 11665408 | tf_op jit(solution)/shard_map/back_to_rows/pallas_call | solution.py:63
  355.0 6.9 %back_to_rows.10 = (f32[192,1024]{1,0:T(8,128)}, f32[192,1024]{1,0:T(8,128)}) custom-call(bf16[96,3584]{1,0:T(8,128)(2,1)} %get-tuple-element.45.refs_0_.refs_1_, bf16[96,3584]{1,0:T(8,128)(2,1)} %copy-done.8, bf16[96,3584]{1,0:T(8,128)(2,1)} %copy-done.25, bf16[96,3584]{1,0:T(8,128)(2,1)} %copy-done.11, bf16[2,1024,3584]{2,1,0:T(8,128)(2,1)} %refs_4_.10), custom_call_target="tpu_custom_call" | custom-call | flops 2818572288 | bytes 11665408 | tf_op jit(solution)/shard_map/back_to_rows/pallas_call | solution.py:63
  363.0 7.7 %back_to_rows.11 = (f32[192,1024]{1,0:T(8,128)}, f32[192,1024]{1,0:T(8,128)}) custom-call(bf16[96,3584]{1,0:T(8,128)(2,1)} %get-tuple-element.44.refs_0_.refs_1_, bf16[96,3584]{1,0:T(8,128)(2,1)} %collective-permute-done.41.refs_8_.refs_9_.refs_1_.refs_2_, bf16[96,3584]{1,0:T(8,128)(2,1)} %copy-done.29, bf16[96,3584]{1,0:T(8,128)(2,1)} %copy-done.30, ...), custom_call_target="tpu_custom_call" | custom-call | flops 2818572288 | bytes 11665408 | tf_op jit(solution)/shard_map/back_to_rows/pallas_call | solution.py:63
  379.4 7.8 %outer.10.refs_5_ = bf16[2,1024,3584]{2,1,0:T(8,128)(2,1)} custom-call(bf16[1024,384]{1,0:T(8,128)(2,1)} %bitcast.127, bf16[96,3584]{1,0:T(8,128)(2,1)} %get-tuple-element.41.refs_0_.refs_1_, bf16[96,3584]{1,0:T(8,128)(2,1)} %copy-done.13, bf16[96,3584]{1,0:T(8,128)(2,1)} %copy-done.26, bf16[96,3584]{1,0:T(8,128)(2,1)} %copy-done.27, ...), custom_call_target="tpu_custom_call" | custom-call | tf_op jit(solution)/shard_map/outer/pallas_call | solution.py:94
  387.2 7.8 %outer.11.refs_4_ = bf16[2,1024,3584]{2,1,0:T(8,128)(2,1)} custom-call(bf16[1024,384]{1,0:T(8,128)(2,1)} %bitcast.129, bf16[96,3584]{1,0:T(8,128)(2,1)} %get-tuple-element.44.refs_0_.refs_1_, bf16[96,3584]{1,0:T(8,128)(2,1)} %collective-permute-done.41.refs_8_.refs_9_.refs_1_.refs_2_, bf16[96,3584]{1,0:T(8,128)(2,1)} %copy-done.29, ...), custom_call_target="tpu_custom_call", output_to_operand_aliasing={{}: (5, {})} | custom-call | tf_op jit(solution)/shard_map/outer/pallas_call | solution.py:94
  (263 shorter events, 175.6 us)
Async XLA Ops:
  45.1 68.4 %collective-permute-start.4 = (bf16[192,3584]{1,0:T(8,128)(2,1)}, bf16[192,3584]{1,0:T(8,128)(2,1)}, u32[]{:S(2)}, u32[]{:S(2)}) collective-permute-start(bf16[192,3584]{1,0:T(8,128)(2,1)} %fusion.36.refs_1_), channel_id=1, source_target_pairs={{0,8},{8,0},{16,24},{24,16},{1,9},{9,1},{17,25},{25,17},{2,10},{10... | collective-permute-start | bytes 4128776 | tf_op jit(solution)/shard_map/ppermute | solution.py:171
  45.5 63.5 %collective-permute-start.17 = (bf16[192,3584]{1,0:T(8,128)(2,1)}, bf16[192,3584]{1,0:T(8,128)(2,1)}, u32[]{:S(2)}, u32[]{:S(2)}) collective-permute-start(bf16[192,3584]{1,0:T(8,128)(2,1)} %fusion.39.refs_2_), channel_id=1, source_target_pairs={{0,16},{8,24},{16,0},{24,8},{1,17},{9,25},{17,1},{25,9},{2,18},{10... | collective-permute-start | bytes 4128776 | tf_op jit(solution)/shard_map/ppermute | solution.py:171
  67.3 44.3 %collective-permute-start.6 = (bf16[192,3584]{1,0:T(8,128)(2,1)}, bf16[192,3584]{1,0:T(8,128)(2,1)}, u32[]{:S(2)}, u32[]{:S(2)}) collective-permute-start(bf16[192,3584]{1,0:T(8,128)(2,1)} %fusion.42), channel_id=1, source_target_pairs={{0,8},{8,0},{16,24},{24,16},{1,9},{9,1},{17,25},{25,17},{2,10},{10... | collective-permute-start | bytes 4128776 | tf_op jit(solution)/shard_map/ppermute | solution.py:171
  71.1 35.2 %collective-permute-start.19 = (bf16[192,3584]{1,0:T(8,128)(2,1)}, bf16[192,3584]{1,0:T(8,128)(2,1)}, u32[]{:S(2)}, u32[]{:S(2)}) collective-permute-start(bf16[192,3584]{1,0:T(8,128)(2,1)} %fusion.45), channel_id=1, source_target_pairs={{0,16},{8,24},{16,0},{24,8},{1,17},{9,25},{17,1},{25,9},{2,18},{10... | collective-permute-start | bytes 4128776 | tf_op jit(solution)/shard_map/ppermute | solution.py:171
  89.7 48.4 %collective-permute-start.15 = (bf16[192,3584]{1,0:T(8,128)(2,1)S(1)}, bf16[192,3584]{1,0:T(8,128)(2,1)S(1)}, u32[]{:S(2)}, u32[]{:S(2)}) collective-permute-start(bf16[192,3584]{1,0:T(8,128)(2,1)S(1)} %fusion.48), channel_id=1, source_target_pairs={{0,8},{8,0},{16,24},{24,16},{1,9},{9,1},{17,25},{25,17},{2,10},{10... | collective-permute-start | bytes 4128776 | tf_op jit(solution)/shard_map/ppermute | solution.py:171
  106.3 30.1 %collective-permute-start.24 = (bf16[192,3584]{1,0:T(8,128)(2,1)S(1)}, bf16[192,3584]{1,0:T(8,128)(2,1)S(1)}, u32[]{:S(2)}, u32[]{:S(2)}) collective-permute-start(bf16[192,3584]{1,0:T(8,128)(2,1)S(1)} %fusion.51), channel_id=1, source_target_pairs={{0,16},{8,24},{16,0},{24,8},{1,17},{9,25},{17,1},{25,9},{2,18},{10... | collective-permute-start | bytes 4128776 | tf_op jit(solution)/shard_map/ppermute | solution.py:171
  109.0 41.5 %collective-permute-start.20 = (bf16[96,3584]{1,0:T(8,128)(2,1)S(1)}, bf16[96,3584]{1,0:T(8,128)(2,1)S(1)}, u32[]{:S(2)}, u32[]{:S(2)}) collective-permute-start(bf16[96,3584]{1,0:T(8,128)(2,1)S(1)} %fusion.76), channel_id=1, source_target_pairs={{0,8},{8,0},{16,24},{24,16},{1,9},{9,1},{17,25},{25,17},{2,10},{10... | collective-permute-start | bytes 2064392 | tf_op jit(solution)/shard_map/ppermute | solution.py:171
  111.6 53.7 %collective-permute-start.18 = (bf16[96,3584]{1,0:T(8,128)(2,1)S(1)}, bf16[96,3584]{1,0:T(8,128)(2,1)S(1)}, u32[]{:S(2)}, u32[]{:S(2)}) collective-permute-start(bf16[96,3584]{1,0:T(8,128)(2,1)S(1)} %fusion.78), channel_id=1, source_target_pairs={{0,8},{8,0},{16,24},{24,16},{1,9},{9,1},{17,25},{25,17},{2,10},{10... | collective-permute-start | bytes 2064392 | tf_op jit(solution)/shard_map/ppermute | solution.py:171
  113.5 70.4 %collective-permute-start.7 = (bf16[96,3584]{1,0:T(8,128)(2,1)S(1)}, bf16[96,3584]{1,0:T(8,128)(2,1)S(1)}, u32[]{:S(2)}, u32[]{:S(2)}) collective-permute-start(bf16[96,3584]{1,0:T(8,128)(2,1)S(1)} %fusion.82), channel_id=1, source_target_pairs={{0,16},{8,24},{16,0},{24,8},{1,17},{9,25},{17,1},{25,9},{2,18},{10... | collective-permute-start | bytes 2064392 | tf_op jit(solution)/shard_map/ppermute | solution.py:171
  136.4 47.6 %collective-permute-start.5 = (bf16[96,3584]{1,0:T(8,128)(2,1)S(1)}, bf16[96,3584]{1,0:T(8,128)(2,1)S(1)}, u32[]{:S(2)}, u32[]{:S(2)}) collective-permute-start(bf16[96,3584]{1,0:T(8,128)(2,1)S(1)} %fusion.84), channel_id=1, source_target_pairs={{0,16},{8,24},{16,0},{24,8},{1,17},{9,25},{17,1},{25,9},{2,18},{10... | collective-permute-start | bytes 2064392 | tf_op jit(solution)/shard_map/ppermute | solution.py:171
  138.1 41.9 %collective-permute-start.25 = (bf16[96,3584]{1,0:T(8,128)(2,1)S(1)}, bf16[96,3584]{1,0:T(8,128)(2,1)S(1)}, u32[]{:S(2)}, u32[]{:S(2)}) collective-permute-start(bf16[96,3584]{1,0:T(8,128)(2,1)S(1)} %fusion.74), channel_id=1, source_target_pairs={{0,8},{8,0},{16,24},{24,16},{1,9},{9,1},{17,25},{25,17},{2,10},{10... | collective-permute-start | bytes 2064392 | tf_op jit(solution)/shard_map/ppermute | solution.py:171
  150.5 33.5 %collective-permute-start.16 = (bf16[96,3584]{1,0:T(8,128)(2,1)S(1)}, bf16[96,3584]{1,0:T(8,128)(2,1)S(1)}, u32[]{:S(2)}, u32[]{:S(2)}) collective-permute-start(bf16[96,3584]{1,0:T(8,128)(2,1)S(1)} %fusion.80), channel_id=1, source_target_pairs={{0,16},{8,24},{16,0},{24,8},{1,17},{9,25},{17,1},{25,9},{2,18},{10... | collective-permute-start | bytes 2064392 | tf_op jit(solution)/shard_map/ppermute | solution.py:171
  204.5 29.8 %collective-permute-start.30 = (bf16[96,3584]{1,0:T(8,128)(2,1)}, bf16[96,3584]{1,0:T(8,128)(2,1)}, u32[]{:S(2)}, u32[]{:S(2)}) collective-permute-start(bf16[96,3584]{1,0:T(8,128)(2,1)} %get-tuple-element.46.refs_0_.refs_1_), channel_id=1, source_target_pairs={{0,16},{8,24},{16,0},{24,8},{1,17},{9,25},{17,1},{25,9},{2,18},{10... | collective-permute-start | bytes 2064392 | tf_op jit(solution)/shard_map/ppermute | solution.py:171
  226.0 35.9 %collective-permute-start.9 = (bf16[96,3584]{1,0:T(8,128)(2,1)}, bf16[96,3584]{1,0:T(8,128)(2,1)}, u32[]{:S(2)}, u32[]{:S(2)}) collective-permute-start(bf16[96,3584]{1,0:T(8,128)(2,1)} %get-tuple-element.43.refs_0_.refs_1_), channel_id=1, source_target_pairs={{0,8},{8,0},{16,24},{24,16},{1,9},{9,1},{17,25},{25,17},{2,10},{10... | collective-permute-start | bytes 2064392 | tf_op jit(solution)/shard_map/ppermute | solution.py:171
  226.3 43.7 %collective-permute-start.41 = (bf16[96,3584]{1,0:T(8,128)(2,1)}, bf16[96,3584]{1,0:T(8,128)(2,1)}, u32[]{:S(2)}, u32[]{:S(2)}) collective-permute-start(bf16[96,3584]{1,0:T(8,128)(2,1)} %get-tuple-element.44.refs_0_.refs_1_), channel_id=1, source_target_pairs={{0,8},{8,0},{16,24},{24,16},{1,9},{9,1},{17,25},{25,17},{2,10},{10... | collective-permute-start | bytes 2064392 | tf_op jit(solution)/shard_map/ppermute | solution.py:171
  234.3 45.2 %collective-permute-start.36 = (bf16[96,3584]{1,0:T(8,128)(2,1)S(1)}, bf16[96,3584]{1,0:T(8,128)(2,1)S(1)}, u32[]{:S(2)}, u32[]{:S(2)}) collective-permute-start(bf16[96,3584]{1,0:T(8,128)(2,1)S(1)} %copy-done.15), channel_id=1, source_target_pairs={{0,16},{8,24},{16,0},{24,8},{1,17},{9,25},{17,1},{25,9},{2,18},{10... | collective-permute-start | bytes 2064392 | tf_op jit(solution)/shard_map/ppermute | solution.py:171
  256.2 38.4 %collective-permute-start.31 = (f32[192,1024]{1,0:T(8,128)}, f32[192,1024]{1,0:T(8,128)S(1)}, u32[]{:S(2)}, u32[]{:S(2)}) collective-permute-start(f32[192,1024]{1,0:T(8,128)} %get-tuple-element.32), channel_id=1, source_target_pairs={{0,1},{1,0},{2,3},{3,2},{4,5},{5,4},{6,7},{7,6},{8,9},{9,8},{10,11... | collective-permute-start | bytes 2359304 | tf_op jit(solution)/shard_map/ppermute | solution.py:177
  260.7 28.0 %collective-permute-start.27 = (bf16[96,3584]{1,0:T(8,128)(2,1)}, bf16[96,3584]{1,0:T(8,128)(2,1)S(1)}, u32[]{:S(2)}, u32[]{:S(2)}) collective-permute-start(bf16[96,3584]{1,0:T(8,128)(2,1)} %copy-done.9), channel_id=1, source_target_pairs={{0,8},{8,0},{16,24},{24,16},{1,9},{9,1},{17,25},{25,17},{2,10},{10... | collective-permute-start | bytes 2064392 | tf_op jit(solution)/shard_map/ppermute | solution.py:171
  279.6 35.9 %collective-permute-start.39 = (bf16[96,3584]{1,0:T(8,128)(2,1)}, bf16[96,3584]{1,0:T(8,128)(2,1)S(1)}, u32[]{:S(2)}, u32[]{:S(2)}) collective-permute-start(bf16[96,3584]{1,0:T(8,128)(2,1)} %held.6), channel_id=1, source_target_pairs={{0,8},{8,0},{16,24},{24,16},{1,9},{9,1},{17,25},{25,17},{2,10},{10... | collective-permute-start | bytes 2064392 | tf_op jit(solution)/shard_map/ppermute | solution.py:171
  288.7 44.2 %collective-permute-start.40 = (bf16[96,3584]{1,0:T(8,128)(2,1)}, bf16[96,3584]{1,0:T(8,128)(2,1)S(1)}, u32[]{:S(2)}, u32[]{:S(2)}) collective-permute-start(bf16[96,3584]{1,0:T(8,128)(2,1)} %held.7), channel_id=1, source_target_pairs={{0,16},{8,24},{16,0},{24,8},{1,17},{9,25},{17,1},{25,9},{2,18},{10... | collective-permute-start | bytes 2064392 | tf_op jit(solution)/shard_map/ppermute | solution.py:171
  307.8 54.1 %collective-permute-start.43 = (bf16[96,3584]{1,0:T(8,128)(2,1)S(1)}, bf16[96,3584]{1,0:T(8,128)(2,1)S(1)}, u32[]{:S(2)}, u32[]{:S(2)}) collective-permute-start(bf16[96,3584]{1,0:T(8,128)(2,1)S(1)} %copy-done.16), channel_id=1, source_target_pairs={{0,16},{8,24},{16,0},{24,8},{1,17},{9,25},{17,1},{25,9},{2,18},{10... | collective-permute-start | bytes 2064392 | tf_op jit(solution)/shard_map/ppermute | solution.py:171
  313.9 29.6 %collective-permute-start.37 = (bf16[96,3584]{1,0:T(8,128)(2,1)S(1)}, bf16[96,3584]{1,0:T(8,128)(2,1)S(1)}, u32[]{:S(2)}, u32[]{:S(2)}) collective-permute-start(bf16[96,3584]{1,0:T(8,128)(2,1)S(1)} %copy-done.15), channel_id=1, source_target_pairs={{0,8},{8,0},{16,24},{24,16},{1,9},{9,1},{17,25},{25,17},{2,10},{10... | collective-permute-start | bytes 2064392 | tf_op jit(solution)/shard_map/ppermute | solution.py:171
  314.9 28.7 %collective-permute-start.38 = (bf16[96,3584]{1,0:T(8,128)(2,1)S(1)}, bf16[96,3584]{1,0:T(8,128)(2,1)S(1)}, u32[]{:S(2)}, u32[]{:S(2)}) collective-permute-start(bf16[96,3584]{1,0:T(8,128)(2,1)S(1)} %copy-done.14), channel_id=1, source_target_pairs={{0,8},{8,0},{16,24},{24,16},{1,9},{9,1},{17,25},{25,17},{2,10},{10... | collective-permute-start | bytes 2064392 | tf_op jit(solution)/shard_map/ppermute | solution.py:171
  332.9 29.0 %collective-permute-start.44 = (bf16[96,3584]{1,0:T(8,128)(2,1)}, bf16[96,3584]{1,0:T(8,128)(2,1)S(1)}, u32[]{:S(2)}, u32[]{:S(2)}) collective-permute-start(bf16[96,3584]{1,0:T(8,128)(2,1)} %collective-permute-done.41.refs_8_.refs_9_.refs_1_.refs_2_), channel_id=1, source_target_pairs={{0,16},{8,24},{16,0},{24,8},{1,17},{9,25},{17,1},{25,9},{2,18},{10... | collective-permute-start | bytes 2064392 | tf_op jit(solution)/shard_map/ppermute | solution.py:171
  (74 other events, 761.3 us)
